TPU v7x, 128 devices: a whole 4x4x4 slice. The times are simulated.
128 devices in a mesh: fsdp: 32 (over y, z_hi, x), tensor: 4 (over z_lo, core).
Axes of the slice: x: 4, y: 4, z: 4 (z_hi: 2, z_lo: 2; z = z_hi * 2 + z_lo), core: 2. Of those that a mesh axis runs over, the one named last changes fastest.
Arguments:
- images: bfloat16 [256, 14, 14, 512], P('fsdp'), may hold values from -6 to 6
- out_grad: bfloat16 [256, 14, 14, 512], P('fsdp'), may hold values from -6 to 6
- rel_index: int32 [49, 49], replicated, may hold values from 0 to 168
- attn_weight: float32 [512, 3, 512], P('fsdp', None, 'tensor'), may hold values from -0.25 to 0.25
- attn_first: float32 [512, 3, 512], P('fsdp', None, 'tensor'), may hold values from -112 to 112
- attn_second: float32 [512, 3, 512], P('fsdp', None, 'tensor'), may hold values from 25.088 to 100.352
- proj_weight: float32 [512, 512], P('tensor', 'fsdp'), may hold values from -1 to 1
- proj_first: float32 [512, 512], P('tensor', 'fsdp'), may hold values from -32 to 32
- proj_second: float32 [512, 512], P('tensor', 'fsdp'), may hold values from 3.01056 to 12.04224
- up_weight: float32 [512, 2048], P('fsdp', 'tensor'), may hold values from -0.25 to 0.25
- up_first: float32 [512, 2048], P('fsdp', 'tensor'), may hold values from -48 to 48
- up_second: float32 [512, 2048], P('fsdp', 'tensor'), may hold values from 4.51584 to 18.06336
- down_weight: float32 [2048, 512], P('tensor', 'fsdp'), may hold values from -0.125 to 0.125
- down_first: float32 [2048, 512], P('tensor', 'fsdp'), may hold values from -96 to 96
- down_second: float32 [2048, 512], P('tensor', 'fsdp'), may hold values from 18.06336 to 72.25344
- vectors: float32 [6, 512], replicated, may hold values from -4 to 4
- vec_first: float32 [6, 512], replicated, may hold values from -160 to 160
- vec_second: float32 [6, 512], replicated, may hold values from 50.176 to 200.704
- head_bias: float32 [2, 512], P(None, 'tensor'), may hold values from -4 to 4
- head_first: float32 [2, 512], P(None, 'tensor'), may hold values from -112 to 112
- head_second: float32 [2, 512], P(None, 'tensor'), may hold values from 25.088 to 100.352
- unit_bias: float32 [2048], P('tensor'), may hold values from -4 to 4
- unit_first: float32 [2048], P('tensor'), may hold values from -48 to 48
- unit_second: float32 [2048], P('tensor'), may hold values from 4.51584 to 18.06336
- rel_table: float32 [169, 16], P(None, 'tensor'), may hold values from -6 to 6
- table_first: float32 [169, 16], P(None, 'tensor'), may hold values from -40 to 40
- table_second: float32 [169, 16], P(None, 'tensor'), may hold values from 3.51232 to 14.04928
Outputs:
- block_out: bfloat16 [256, 14, 14, 512], P('fsdp')
- images_grad: float32 [256, 14, 14, 512], P('fsdp')
- attn_new: float32 [512, 3, 512], P('fsdp', None, 'tensor')
- attn_moment: float32 [512, 3, 512], P('fsdp', None, 'tensor')
- attn_square: float32 [512, 3, 512], P('fsdp', None, 'tensor')
- proj_new: float32 [512, 512], P('tensor', 'fsdp')
- proj_moment: float32 [512, 512], P('tensor', 'fsdp')
- proj_square: float32 [512, 512], P('tensor', 'fsdp')
- up_new: float32 [512, 2048], P('fsdp', 'tensor')
- up_moment: float32 [512, 2048], P('fsdp', 'tensor')
- up_square: float32 [512, 2048], P('fsdp', 'tensor')
- down_new: float32 [2048, 512], P('tensor', 'fsdp')
- down_moment: float32 [2048, 512], P('tensor', 'fsdp')
- down_square: float32 [2048, 512], P('tensor', 'fsdp')
- vec_new: float32 [6, 512], replicated
- vec_moment: float32 [6, 512], replicated
- vec_square: float32 [6, 512], replicated
- head_new: float32 [2, 512], P(None, 'tensor')
- head_moment: float32 [2, 512], P(None, 'tensor')
- head_square: float32 [2, 512], P(None, 'tensor')
- unit_new: float32 [2048], P('tensor')
- unit_moment: float32 [2048], P('tensor')
- unit_square: float32 [2048], P('tensor')
- table_new: float32 [169, 16], P(None, 'tensor')
- table_moment: float32 [169, 16], P(None, 'tensor')
- table_square: float32 [169, 16], P(None, 'tensor')
Inputs may be any that keep to these rules, and one draw needn't show every extreme that they name: `rel_index`: each entry names a row of rel_table.
All inputs are finite; a program needn't handle non-finite values.
Results may differ from a plain program's by a relative error of at most 0.012.
Values may be sent and summed in bfloat16 or wider, within the bound.
A program may use at most 128 MiB of HBM per device.

v0:
```python
import jax
import jax.numpy as jnp
from jax import lax
from jax.sharding import PartitionSpec as P

HD = 32
SIDE = 14
WIN = 7
STEP = 10
REL = 169


NORM_EPS = 1e-05
BETA_ONE = 0.9
BETA_TWO = 0.999
ADAM_EPS = 1e-08
RATE_MATRIX = 0.1
RATE_VECTOR = 0.2
RATE_TABLE = 0.5
WEIGHT_DECAY = 0.05


def rows_first(arrays, axis, dims):
    turned = [jnp.moveaxis(a, dim, 0) for a, dim in zip(arrays, dims)]
    widths = [t[0].size for t in turned]
    both = jnp.concatenate([t.reshape(-1, w) for t, w in zip(turned, widths)], axis=1)
    result = lax.all_gather(both, axis, axis=0, tiled=True)
    parts = jnp.split(result, [sum(widths[:k]) for k in range(1, len(widths))], axis=1)
    return tuple(
        (
            jnp.moveaxis(b.reshape(-1, *t.shape[1:]), 0, dim)
            for b, t, dim in zip(parts, turned, dims)
        )
    )


def sent_to_all(value, axis):
    peers = lax.axis_size(axis)
    return lax.all_to_all(
        jnp.broadcast_to(value[None], (peers, *value.shape)), axis, 0, 0, tiled=True
    )


def taken_together(value, axis):
    everything = sent_to_all(value, axis)
    return jnp.sum(everything, axis=0)


def in_one(arrays, axis):
    ends = [0]
    for a in arrays:
        ends.append(ends[-1] + a.size)
    so_far = taken_together(jnp.concatenate([a.ravel() for a in arrays]), axis)
    return tuple((so_far[b:e].reshape(a.shape) for a, b, e in zip(arrays, ends, ends[1:])))


def cut_along(value, dim, peers):
    lengths = value.shape
    parts = value.reshape(*lengths[:dim], peers, lengths[dim] // peers, *lengths[dim + 1 :])
    return jnp.moveaxis(parts, dim, 0)


def sum_together(arrays, axis, dims):
    peers = lax.axis_size(axis)
    parts = [cut_along(a, dim, peers) for a, dim in zip(arrays, dims)]
    lines = jnp.concatenate([b.reshape(peers, -1) for b in parts], axis=1)
    span = max(16, -(-lines.shape[1] // 1024) * 8)
    lines = jnp.pad(lines, ((0, 0), (0, span * 128 - lines.shape[1]))).reshape(-1, 128)
    line, at, outs = (lax.psum_scatter(lines, axis, tiled=True).reshape(-1), 0, [])
    for b in parts:
        part = b[0]
        outs.append(line[at : at + part.size].reshape(part.shape))
        at += part.size
    return tuple(outs)


def layer_norm(values, offset, shift):
    center = values - jnp.mean(values, axis=-1, keepdims=True)
    spread = jnp.mean(center * center, axis=-1, keepdims=True)
    return center * lax.rsqrt(spread + NORM_EPS) * (1.0 + offset) + shift


def exact_gelu(values):
    return jax.nn.gelu(values, approximate=False)


def to_windows(field):
    count = field.shape[0]
    split = field.reshape(count, SIDE // WIN, WIN, SIDE // WIN, WIN, field.shape[-1])
    return split.transpose(0, 1, 3, 2, 4, 5).reshape(-1, WIN * WIN, field.shape[-1])


def from_windows(field, count):
    split = field.reshape(count, SIDE // WIN, SIDE // WIN, WIN, WIN, field.shape[-1])
    return split.transpose(0, 1, 3, 2, 4, 5).reshape(count, SIDE, SIDE, field.shape[-1])


def adam_step(weight, grad, first, second, rate, decay):
    first_new = BETA_ONE * first + (1.0 - BETA_ONE) * grad
    second_new = BETA_TWO * second + (1.0 - BETA_TWO) * grad * grad
    first_hat = first_new / (1.0 - BETA_ONE**STEP)
    second_hat = second_new / (1.0 - BETA_TWO**STEP)
    updated = weight - rate * (first_hat / (jnp.sqrt(second_hat) + ADAM_EPS) + decay * weight)
    return (updated, first_new, second_new)


def on_device(
    images,
    out_grad,
    rel_index,
    attn_weight,
    attn_first,
    attn_second,
    proj_weight,
    proj_first,
    proj_second,
    up_weight,
    up_first,
    up_second,
    down_weight,
    down_first,
    down_second,
    vectors,
    vec_first,
    vec_second,
    head_bias,
    head_first,
    head_second,
    unit_bias,
    unit_first,
    unit_second,
    rel_table,
    table_first,
    table_second,
):
    low_type = jnp.bfloat16
    full_type = jnp.float32
    highest = lax.Precision.HIGHEST
    images_count = images.shape[0]
    heads_dev = rel_table.shape[1]
    score_scale = float(HD) ** (-0.5)
    full_attn, full_proj, full_up, full_down = rows_first(
        (
            attn_weight.astype(low_type),
            proj_weight.astype(low_type),
            up_weight.astype(low_type),
            down_weight.astype(low_type),
        ),
        "fsdp",
        (0, 1, 0, 1),
    )
    tokens = to_windows(images.astype(full_type))
    windows = tokens.shape[0]
    window_len = WIN * WIN
    heads_shape = (windows, window_len, heads_dev, HD)
    norm_one, pull_one = jax.vjp(layer_norm, tokens, vectors[0], vectors[1])
    norm_one_low = norm_one.astype(low_type)
    mixed = jnp.einsum("wtd,dce->wtce", norm_one_low, full_attn, preferred_element_type=full_type)
    query_low = (mixed[:, :, 0] + head_bias[0]).astype(low_type).reshape(heads_shape)
    keys_low = mixed[:, :, 1].astype(low_type).reshape(heads_shape)
    values_low = (mixed[:, :, 2] + head_bias[1]).astype(low_type).reshape(heads_shape)
    onehot = (rel_index[:, :, None] == jnp.arange(REL, dtype=jnp.int32)[None, None, :]).astype(
        full_type
    )
    pos_bias = jnp.einsum("qkr,rh->hqk", onehot, rel_table, precision=highest)

    def scores_of(queries, keyset):
        raw = jnp.einsum("wqhe,wkhe->whqk", queries, keyset, preferred_element_type=full_type)
        return raw * score_scale + pos_bias

    scores = scores_of(query_low, keys_low)
    top_score = jnp.max(scores, axis=-1, keepdims=True)
    log_total = top_score + jnp.log(jnp.sum(jnp.exp(scores - top_score), axis=-1, keepdims=True))
    prob_low = jnp.exp(scores - log_total).astype(low_type)
    attended = jnp.einsum("whqk,wkhe->wqhe", prob_low, values_low, preferred_element_type=full_type)
    attended_low = attended.reshape(windows, window_len, heads_dev * HD).astype(low_type)
    branch_part = jnp.einsum(
        "wte,ed->wtd", attended_low, full_proj, preferred_element_type=full_type
    )
    branch = lax.psum(branch_part, "tensor")
    middle = tokens + branch + vectors[2]
    norm_two, pull_two = jax.vjp(layer_norm, middle, vectors[3], vectors[4])
    norm_two_low = norm_two.astype(low_type)
    pre_act = (
        jnp.einsum("wtd,df->wtf", norm_two_low, full_up, preferred_element_type=full_type)
        + unit_bias
    )
    hidden, pull_gelu = jax.vjp(exact_gelu, pre_act)
    hidden_low = hidden.astype(low_type)
    down_part = jnp.einsum("wtf,fd->wtd", hidden_low, full_down, preferred_element_type=full_type)
    result = (middle + lax.psum(down_part, "tensor") + vectors[5]).astype(low_type)
    block_out = from_windows(result, images_count)
    back_attn, back_proj, back_up, back_down = rows_first(
        (
            attn_weight.astype(low_type),
            proj_weight.astype(low_type),
            up_weight.astype(low_type),
            down_weight.astype(low_type),
        ),
        "fsdp",
        (0, 1, 0, 1),
    )
    cot_low = to_windows(out_grad)
    grad_down = jnp.einsum("wtf,wtd->fd", hidden_low, cot_low, preferred_element_type=full_type)
    grad_hidden = jnp.einsum("wtd,fd->wtf", cot_low, back_down, preferred_element_type=full_type)
    grad_pre = pull_gelu(grad_hidden)[0]
    grad_pre_low = grad_pre.astype(low_type)
    grad_unit = jnp.sum(grad_pre, axis=(0, 1))
    grad_up = jnp.einsum(
        "wtd,wtf->df", norm_two_low, grad_pre_low, preferred_element_type=full_type
    )
    norm_two_part = jnp.einsum(
        "wtf,df->wtd", grad_pre_low, back_up, preferred_element_type=full_type
    )
    grad_norm_two = lax.psum(norm_two_part, "tensor")
    grad_mid_norm, grad_g2, grad_b2 = pull_two(grad_norm_two)
    grad_middle = cot_low.astype(full_type) + grad_mid_norm
    grad_middle_low = grad_middle.astype(low_type)
    grad_proj = jnp.einsum(
        "wte,wtd->ed", attended_low, grad_middle_low, preferred_element_type=full_type
    )
    grad_att = jnp.einsum(
        "wtd,ed->wte", grad_middle_low, back_proj, preferred_element_type=full_type
    )
    grad_att = grad_att.astype(low_type).reshape(heads_shape)
    probs_again = jnp.exp(scores_of(query_low, keys_low) - log_total)
    prob_again_low = probs_again.astype(low_type)
    grad_prob = jnp.einsum(
        "wqhe,wkhe->whqk", grad_att, values_low, preferred_element_type=full_type
    )
    grad_values = jnp.einsum(
        "whqk,wqhe->wkhe", prob_again_low, grad_att, preferred_element_type=full_type
    ).astype(low_type)
    grad_scores = probs_again * (
        grad_prob - jnp.sum(grad_prob * probs_again, axis=-1, keepdims=True)
    )
    grad_scores_low = grad_scores.astype(low_type)
    grad_table = jnp.einsum(
        "qkr,hqk->rh", onehot, jnp.sum(grad_scores_low.astype(full_type), axis=0), precision=highest
    )
    grad_query = (
        jnp.einsum("whqk,wkhe->wqhe", grad_scores_low, keys_low, preferred_element_type=full_type)
        * score_scale
    ).astype(low_type)
    grad_keys = (
        jnp.einsum("whqk,wqhe->wkhe", grad_scores_low, query_low, preferred_element_type=full_type)
        * score_scale
    ).astype(low_type)
    grad_head = jnp.stack(
        [
            jnp.sum(grad_query.astype(full_type), axis=(0, 1)).reshape(-1),
            jnp.sum(grad_values.astype(full_type), axis=(0, 1)).reshape(-1),
        ]
    )
    grad_mixed = jnp.stack([grad_query, grad_keys, grad_values], axis=2).reshape(
        windows, window_len, 3, heads_dev * HD
    )
    grad_attn = jnp.einsum(
        "wtd,wtce->dce", norm_one_low, grad_mixed, preferred_element_type=full_type
    )
    norm_one_part = jnp.einsum(
        "wtce,dce->wtd", grad_mixed, back_attn, preferred_element_type=full_type
    )
    grad_norm_one = lax.psum(norm_one_part, "tensor")
    grad_tok_norm, grad_g1, grad_b1 = pull_one(grad_norm_one)
    images_grad = from_windows(grad_middle + grad_tok_norm, images_count)
    grad_vectors = jnp.stack(
        [
            grad_g1,
            grad_b1,
            jnp.sum(grad_middle, axis=(0, 1)),
            grad_g2,
            grad_b2,
            jnp.sum(cot_low.astype(full_type), axis=(0, 1)),
        ]
    )
    vec_grad, head_grad, unit_grad, table_grad = in_one(
        (grad_vectors, grad_head, grad_unit, grad_table), "fsdp"
    )
    attn_grad, proj_grad, up_grad, down_grad = sum_together(
        (grad_attn, grad_proj, grad_up, grad_down), "fsdp", (0, 1, 0, 1)
    )
    attn_out = adam_step(attn_weight, attn_grad, attn_first, attn_second, RATE_MATRIX, WEIGHT_DECAY)
    proj_out = adam_step(proj_weight, proj_grad, proj_first, proj_second, RATE_MATRIX, WEIGHT_DECAY)
    up_out = adam_step(up_weight, up_grad, up_first, up_second, RATE_MATRIX, WEIGHT_DECAY)
    down_out = adam_step(down_weight, down_grad, down_first, down_second, RATE_MATRIX, WEIGHT_DECAY)
    vec_out = adam_step(vectors, vec_grad, vec_first, vec_second, RATE_VECTOR, 0.0)
    head_out = adam_step(head_bias, head_grad, head_first, head_second, RATE_VECTOR, 0.0)
    unit_out = adam_step(unit_bias, unit_grad, unit_first, unit_second, RATE_VECTOR, 0.0)
    table_out = adam_step(rel_table, table_grad, table_first, table_second, RATE_TABLE, 0.0)
    return (
        (block_out, images_grad)
        + attn_out
        + proj_out
        + up_out
        + down_out
        + vec_out
        + head_out
        + unit_out
        + table_out
    )


def solution(mesh):
    in_specs = (
        P("fsdp", None, None, None),
        P("fsdp", None, None, None),
        P(),
        P("fsdp", None, "tensor"),
        P("fsdp", None, "tensor"),
        P("fsdp", None, "tensor"),
        P("tensor", "fsdp"),
        P("tensor", "fsdp"),
        P("tensor", "fsdp"),
        P("fsdp", "tensor"),
        P("fsdp", "tensor"),
        P("fsdp", "tensor"),
        P("tensor", "fsdp"),
        P("tensor", "fsdp"),
        P("tensor", "fsdp"),
        P(),
        P(),
        P(),
        P(None, "tensor"),
        P(None, "tensor"),
        P(None, "tensor"),
        P("tensor"),
        P("tensor"),
        P("tensor"),
        P(None, "tensor"),
        P(None, "tensor"),
        P(None, "tensor"),
    )
    out_specs = (
        P("fsdp", None, None, None),
        P("fsdp", None, None, None),
        P("fsdp", None, "tensor"),
        P("fsdp", None, "tensor"),
        P("fsdp", None, "tensor"),
        P("tensor", "fsdp"),
        P("tensor", "fsdp"),
        P("tensor", "fsdp"),
        P("fsdp", "tensor"),
        P("fsdp", "tensor"),
        P("fsdp", "tensor"),
        P("tensor", "fsdp"),
        P("tensor", "fsdp"),
        P("tensor", "fsdp"),
        P(),
        P(),
        P(),
        P(None, "tensor"),
        P(None, "tensor"),
        P(None, "tensor"),
        P("tensor"),
        P("tensor"),
        P("tensor"),
        P(None, "tensor"),
        P(None, "tensor"),
        P(None, "tensor"),
    )
    return jax.shard_map(
        on_device, mesh=mesh, in_specs=in_specs, out_specs=out_specs, check_vma=False
    )
```

profile of v0, /device:TPU:1, one launch (start us, length us, event | category | flops | bytes accessed | tf_op | source)
XLA Modules:
  0.0 762.6 jit_solution(15558718354515804666)
XLA Ops:
  10.9 1.9 convert.7
  12.8 4.0 fusion.74
  16.8 1.7 copy.499
  19.9 5.5 multiply_reduce_fusion.6
  25.4 1.7 copy.501
  27.8 2.3 copy.502
  30.7 5.2 add_convert_fusion.3
  35.9 3.8 convert_element_type.108
  39.8 2.0 fusion.43
  42.0 40.1 %all-gather.2.cloned.1.call-done = bf16[512,1536]{1,0:T(8,128)(2,1)} async-done(((bf16[16,1536]{1,0:T(8,128)(2,1)}), bf16[512,1536]{1,0:T(8,128)(2,1)}) %all-gather.2.cloned.1.call-update) | async-done | bytes 1572880 | tf_op jit(solution)/shard_map/all_gather | solution.py:27
  87.1 1.8 copy.509
  88.9 3.6 copy.507
  98.0 3.8 fusion.58
  102.4 2.9 copy.645
  105.3 4.0 reshape.293
  109.3 4.4 copy.647
  113.7 4.7 reshape.299
  118.3 65.5 %all-reduce.5.cloned.1.call-done = f32[32,49,512]{2,1,0:T(8,128)} async-done(((f32[32,49,512]{2,1,0:T(8,128)}), f32[32,49,512]{2,1,0:T(8,128)}) %all-reduce.5.cloned.1.call-update) | async-done | bytes 3211280 | tf_op jit(solution)/shard_map/psum | solution.py:180
  183.9 4.0 fusion.87
  188.7 1.8 copy-done.20
  190.5 2.5 convert_reduce_fusion.1
  193.0 9.0 %multiply_convert_fusion.1 = (bf16[32,49,512]{2,1,0:T(8,128)(2,1)}, f32[32,49,512]{2,1,0:T(8,128)S(1)}) fusion(f32[32,49,512]{2,1,0:T(8,128)S(1)} %get-tuple-element.220, f32[512]{0:T(512)S(1)} %copy-done.47, u32[49,512]{1,0:T(8,128)S(1)} %get-tuple-element.161, u32[49,512]{1,0:T(8,128)S(1)} %get-tuple-element.160), kind=kLoop, calls=%fused_computation.35 | loop fusion | flops 55394304 | bytes 8230912 | tf_op jit(solution)/shard_map/convert_element_type | solution.py:189
  202.0 4.5 fusion.92
  207.7 3.0 fusion.49
  210.8 4.6 fusion.54
  215.4 79.5 %all-reduce.7.cloned.1.call-done = f32[32,49,512]{2,1,0:T(8,128)} async-done(((f32[32,49,512]{2,1,0:T(8,128)}), f32[32,49,512]{2,1,0:T(8,128)}) %all-reduce.7.cloned.1.call-update) | async-done | bytes 3211280 | tf_op jit(solution)/shard_map/psum | solution.py:215
  294.9 5.0 fusion.75
  300.2 1.8 multiply_reduce_fusion
  302.1 3.1 fusion.81
  305.2 1.9 copy-done.5
  307.1 2.4 convolution_convert_fusion.2
  309.4 2.4 copy.520
  311.8 4.8 multiply_reduce_fusion.3
  316.7 2.0 convert_reduce_fusion.2
  318.7 1.7 convert_reduce_fusion.5
  320.4 2.2 multiply_convert_fusion.2
  322.5 2.1 convert_reduce_fusion.4
  324.7 2.4 copy.524
  327.0 2.4 copy.525
  329.4 2.4 copy.526
  331.9 4.4 convolution_bitcast_fusion
  338.0 8.8 %copy.539 = bf16[512,49,32]{1,2,0:T(8,128)(2,1)} copy(bf16[512,49,32]{0,2,1:T(8,128)(2,1)} %bitcast.187) | data formatting | bytes 3211264 | tf_op jit(solution)/shard_map/wtf,wtd->fd/dot_general | solution.py:204
  346.7 5.7 convolution_bitcast_fusion.1
  352.4 2.4 reshape_reshape.7
  354.8 8.3 %fusion.32 = f32[32,512,16]{1,0,2:T(8,128)} fusion(bf16[32,16,49,32]{2,3,1,0:T(8,128)(2,1)} %bitcast.205, bf16[32,49,512]{2,1,0:T(8,128)(2,1)} %get-tuple-element.198), kind=kOutput, calls=%fused_computation.85 | convolution fusion | flops 822083584 | bytes 4259840 | tf_op jit(solution)/shard_map/wtf,wtd->fd/dot_general | solution.py:204
  363.1 4.6 copy.541
  367.8 3.6 copy.543
  371.4 109.0 %all-reduce.9.cloned.1.call-done = (f32[32,49,512]{2,1,0:T(8,128)}, f32[32,49,512]{2,1,0:T(8,128)}) async-done(((f32[32,49,512]{2,1,0:T(8,128)}, f32[32,49,512]{2,1,0:T(8,128)}), (f32[32,49,512]{2,1,0:T(8,128)}, f32[32,49,512]{2,1,0:T(8,128)})) %all-reduce.9.cloned.1.call-update) | async-done | bytes 6422544 | tf_op jit(solution)/shard_map/psum | solution.py:191
  480.4 7.6 fusion.76
  488.1 2.9 fusion.37
  490.9 3.7 multiply_reduce_fusion.1
  496.1 2.4 reshape_reshape.6
  498.5 8.0 %convert_bitcast_fusion = (bf16[512,49,32]{0,1,2:T(8,128)(2,1)}, f32[32,49,512]{2,1,0:T(8,128)}) fusion(f32[32,49,512]{2,1,0:T(8,128)} %copy-done.5, f32[32,49]{1,0:T(8,128)S(1)} %negate_multiply_fusion.1, f32[32,49]{1,0:T(8,128)S(1)} %get-tuple-element.210, f32[32,49]{1,0:T(8,128)S(1)} %div.165, f32[32,49,512]{2,0,1:T(8,128)S(1)} %reshape.293, ...), kind=kLoop, calls=%fused_computation.93 | loop fusion | flops 7225344 | bytes 14477824 | tf_op jit(solution)/shard_map/wte,wtd->ed/dot_general | solution.py:219
  506.5 8.2 %copy.535 = bf16[512,49,32]{1,2,0:T(8,128)(2,1)} copy(bf16[512,49,32]{0,1,2:T(8,128)(2,1)} %get-tuple-element.202) | data formatting | bytes 3211264 | tf_op jit(solution)/shard_map/wte,wtd->ed/dot_general | solution.py:219
  514.7 4.5 fusion.40
  520.0 2.0 pad_maximum_fusion
  522.0 2.2 reshape.305
  527.3 3.4 fusion.44
  532.1 9.1 %all-to-all-start = ((f32[32,1,4516]{2,1,0:T(1,128)}), f32[32,1,4516]{2,1,0:T(1,128)S(1)}, u32[]{:S(2)}, u32[]{:S(2)}) async-start(f32[32,1,4516]{2,1,0:T(1,128)} %broadcast_in_dim.14), calls=%async_computation.1 | async-start | bytes 1179648 | tf_op jit(solution)/shard_map/all_to_all | solution.py:39
  541.2 4.9 reshape.334
  546.1 4.5 copy.644
  550.6 2.7 copy.532
  555.0 3.3 copy.646
  563.0 187.6 %reduce-scatter.2.cloned.1.call-done = f32[192,128]{1,0:T(8,128)} async-done(((f32[6144,128]{1,0:T(8,128)}), f32[192,128]{1,0:T(8,128)}) %reduce-scatter.2.cloned.1.call-update) | async-done | bytes 98320 | tf_op jit(solution)/shard_map/reduce_scatter | solution.py:69
  (215 shorter events, 39.7 us)
Async XLA Ops:
  7.2 74.8 %all-gather.2.cloned.1.call-start = ((), (), s32[]{:S(2)}) async-start(), calls=%async_computation.2 | async-start | bytes 1622016 | tf_op jit(solution)/shard_map/all_gather | solution.py:27
  10.9 173.0 %all-reduce.5.cloned.1.call-start = ((), (), s32[]{:S(2)}) async-start(), calls=%async_computation.3 | async-start | bytes 7340032 | tf_op jit(solution)/shard_map/psum | solution.py:180
  16.8 13.3 %copy-start.30 = (f32[6,512]{1,0:T(8,128)S(1)}, f32[6,512]{1,0:T(8,128)}, u32[]{:S(2)}) copy-start(f32[6,512]{1,0:T(8,128)} %param.42) | copy-start | bytes 36868
  30.7 9.0 %copy-start.49 = (f32[1,512]{1,0:T(1,128)}, f32[1,512]{1,0:T(1,128)S(1)}, u32[]{:S(2)}) copy-start(f32[1,512]{1,0:T(1,128)S(1)} %get-tuple-element.216) | copy-start | bytes 6148
  30.7 9.0 %copy-start.37 = (s32[49,49]{1,0:T(8,128)S(1)}, s32[49,49]{1,0:T(8,128)}, u32[]{:S(2)}) copy-start(s32[49,49]{1,0:T(8,128)} %param.29) | copy-start | bytes 28816
  30.7 9.1 %copy-start.54 = (f32[169,4]{0,1:T(4,128)S(1)}, f32[169,4]{0,1:T(4,128)}, u32[]{:S(2)}) copy-start(f32[169,4]{0,1:T(4,128)} %param.51) | copy-start | bytes 8116
  30.7 11.1 %copy-start.58 = (f32[2,128]{1,0:T(2,128)S(1)}, f32[2,128]{1,0:T(2,128)}, u32[]{:S(2)}) copy-start(f32[2,128]{1,0:T(2,128)} %param.45) | copy-start | bytes 3076
  39.8 42.2 %copy-start.38 = (s32[49,49]{0,1:T(8,128)}, s32[49,49]{0,1:T(8,128)S(1)}, u32[]{:S(2)}) copy-start(s32[49,49]{0,1:T(8,128)S(1)} %copy.510) | copy-start | bytes 28816
  42.0 53.2 %copy-start.42 = (f32[4,32]{1,0:T(4,128)}, f32[4,32]{1,0:T(4,128)S(1)}, u32[]{:S(2)}) copy-start(f32[4,32]{1,0:T(4,128)S(1)} %add.287) | copy-start | bytes 1540
  87.1 6.7 copy-start.7
  88.9 4.9 copy-start.12
  93.8 4.2 copy-start.2
  93.8 2.9 copy-start.9
  98.0 3.9 copy-start.18
  98.0 4.4 copy-start.16
  101.9 193.0 %all-reduce.7.cloned.1.call-start = ((), (), s32[]{:S(2)}) async-start(), calls=%async_computation.4 | async-start | bytes 7340032 | tf_op jit(solution)/shard_map/psum | solution.py:215
  187.9 5.0 copy-start
  187.9 2.6 copy-start.20
  193.0 9.1 %copy-start.10 = (bf16[32,49,512]{2,0,1:T(8,128)(2,1)S(1)}, bf16[32,49,512]{2,0,1:T(8,128)(2,1)}, u32[]{:S(2)}) copy-start(bf16[32,49,512]{2,0,1:T(8,128)(2,1)} %reshape.299) | copy-start | bytes 4816900
  210.7 269.7 %all-reduce.9.cloned.1.call-start = ((), (), s32[]{:S(2)}) async-start(), calls=%async_computation.6 | async-start | bytes 14680064 | tf_op jit(solution)/shard_map/psum | solution.py:191
  294.9 5.1 copy-start.1
  294.9 5.3 copy-start.4
  305.2 6.6 copy-start.43
  311.8 4.8 copy-start.3
  318.7 3.9 copy-start.14
  336.3 10.4 %copy-start.64 = (f32[1,512]{1,0:T(1,128)S(1)}, f32[1,512]{1,0:T(1,128)}, u32[]{:S(2)}) copy-start(f32[1,512]{1,0:T(1,128)} %get-tuple-element.213) | copy-start | bytes 6148
  336.3 414.2 %reduce-scatter.2.cloned.1.call-start = ((), (), s32[]{:S(2)}) async-start(), calls=%async_computation.5 | async-start | bytes 3244032 | tf_op jit(solution)/shard_map/reduce_scatter | solution.py:69
  367.8 112.6 %copy-start.51 = (f32[1,512]{1,0:T(1,128)S(1)}, f32[1,512]{1,0:T(1,128)}, u32[]{:S(2)}) copy-start(f32[1,512]{1,0:T(1,128)} %get-tuple-element.212) | copy-start | bytes 6148
  480.4 7.6 copy-start.23
  480.4 7.6 %copy-start.24 = (bf16[32,49,1,128]{3,1,2,0:T(8,128)(2,1)S(1)}, bf16[32,49,1,128]{3,1,2,0:T(8,128)(2,1)}, u32[]{:S(2)}) copy-start(bf16[32,49,1,128]{3,1,2,0:T(8,128)(2,1)} %copy.525) | copy-start | bytes 1204228
  480.4 7.6 %copy-start.25 = (bf16[32,49,1,128]{3,1,2,0:T(8,128)(2,1)S(1)}, bf16[32,49,1,128]{3,1,2,0:T(8,128)(2,1)}, u32[]{:S(2)}) copy-start(bf16[32,49,1,128]{3,1,2,0:T(8,128)(2,1)} %copy.526) | copy-start | bytes 1204228
  480.4 7.6 %copy-start.50 = (f32[1,512]{1,0:T(1,128)S(1)}, f32[1,512]{1,0:T(1,128)}, u32[]{:S(2)}) copy-start(f32[1,512]{1,0:T(1,128)} %copy-done.49) | copy-start | bytes 6148
  488.1 2.9 copy-start.6
  506.5 8.2 %copy-start.19 = (bf16[32,4,32,49]{3,2,1,0:T(8,128)(2,1)S(1)}, bf16[32,4,32,49]{3,2,1,0:T(8,128)(2,1)}, u32[]{:S(2)}) copy-start(bf16[32,4,32,49]{3,2,1,0:T(8,128)(2,1)} %copy-done.18) | copy-start | bytes 1204228
  524.3 3.0 copy-start.28
  524.3 3.0 copy-start.39
  524.3 6.6 copy-start.46
  524.3 6.6 copy-start.62
  532.1 27.9 %all-to-all-start = ((f32[32,1,4516]{2,1,0:T(1,128)}), f32[32,1,4516]{2,1,0:T(1,128)S(1)}, u32[]{:S(2)}, u32[]{:S(2)}) async-start(f32[32,1,4516]{2,1,0:T(1,128)} %broadcast_in_dim.14), calls=%async_computation.1 | async-start | bytes 1179648 | tf_op jit(solution)/shard_map/all_to_all | solution.py:39
  550.6 2.7 copy-start.15
  554.8 5.7 copy-start.59
  554.8 5.7 copy-start.65
  554.8 5.7 copy-start.66
  554.8 6.3 copy-start.48
  554.8 6.3 copy-start.60
  554.9 6.3 copy-start.61
  554.9 6.9 copy-start.55
  554.9 6.9 copy-start.56
  554.9 6.8 copy-start.57
  554.9 7.5 copy-start.31
  554.9 7.5 copy-start.44
  554.9 7.4 copy-start.45
  554.9 198.2 %copy-start.26 = (f32[512,16]{0,1:T(8,128)S(1)}, f32[512,16]{0,1:T(8,128)}, u32[]{:S(2)}) copy-start(f32[512,16]{0,1:T(8,128)} %param.39) | copy-start | bytes 98308
  555.0 198.2 %copy-start.32 = (f32[512,16]{0,1:T(8,128)S(1)}, f32[512,16]{0,1:T(8,128)}, u32[]{:S(2)}) copy-start(f32[512,16]{0,1:T(8,128)} %param.40) | copy-start | bytes 98308
  555.0 198.2 %copy-start.33 = (f32[512,16]{0,1:T(8,128)S(1)}, f32[512,16]{0,1:T(8,128)}, u32[]{:S(2)}) copy-start(f32[512,16]{0,1:T(8,128)} %param.41) | copy-start | bytes 98308
  555.0 198.9 %copy-start.27 = (f32[16,512]{1,0:T(8,128)S(1)}, f32[16,512]{1,0:T(8,128)}, u32[]{:S(2)}) copy-start(f32[16,512]{1,0:T(8,128)} %param.36) | copy-start | bytes 98308
  555.0 198.9 %copy-start.34 = (f32[16,512]{1,0:T(8,128)S(1)}, f32[16,512]{1,0:T(8,128)}, u32[]{:S(2)}) copy-start(f32[16,512]{1,0:T(8,128)} %param.37) | copy-start | bytes 98308
  555.0 198.9 %copy-start.35 = (f32[16,512]{1,0:T(8,128)S(1)}, f32[16,512]{1,0:T(8,128)}, u32[]{:S(2)}) copy-start(f32[16,512]{1,0:T(8,128)} %param.38) | copy-start | bytes 98308
  558.4 196.2 %copy-start.29 = (f32[16,3,128]{2,0,1:T(8,128)S(1)}, f32[16,3,128]{2,0,1:T(8,128)}, u32[]{:S(2)}) copy-start(f32[16,3,128]{2,0,1:T(8,128)} %param.30) | copy-start | bytes 73732
  558.4 196.2 %copy-start.40 = (f32[16,3,128]{2,0,1:T(8,128)S(1)}, f32[16,3,128]{2,0,1:T(8,128)}, u32[]{:S(2)}) copy-start(f32[16,3,128]{2,0,1:T(8,128)} %param.31) | copy-start | bytes 73732
  558.4 196.2 %copy-start.41 = (f32[16,3,128]{2,0,1:T(8,128)S(1)}, f32[16,3,128]{2,0,1:T(8,128)}, u32[]{:S(2)}) copy-start(f32[16,3,128]{2,0,1:T(8,128)} %param.32) | copy-start | bytes 73732
  558.4 196.8 %copy-start.36 = (f32[128,16]{0,1:T(8,128)S(1)}, f32[128,16]{0,1:T(8,128)}, u32[]{:S(2)}) copy-start(f32[128,16]{0,1:T(8,128)} %param.33) | copy-start | bytes 24580
  558.4 196.8 %copy-start.52 = (f32[128,16]{0,1:T(8,128)S(1)}, f32[128,16]{0,1:T(8,128)}, u32[]{:S(2)}) copy-start(f32[128,16]{0,1:T(8,128)} %param.34) | copy-start | bytes 24580
  558.4 196.8 %copy-start.53 = (f32[128,16]{0,1:T(8,128)S(1)}, f32[128,16]{0,1:T(8,128)}, u32[]{:S(2)}) copy-start(f32[128,16]{0,1:T(8,128)} %param.35) | copy-start | bytes 24580
  (9 other events, 17.6 us)
Sparse Core Ops, SparseCore 0:
  11.0 70.9 all-gather.1
  102.0 81.8 all-reduce.4
  210.8 84.0 all-reduce.6
  336.4 143.9 all-reduce.8
  524.5 226.0 reduce-scatter.1
where the time goes:
time: 769 us; the launch traced here: 763 us
  waiting for transfers between devices  482 us (63%)
  local copies, waits for them, and re-layouts  113 us (15%)
  other arithmetic  76.7 us (10%)
  matrix products  66.6 us (9%)
  between operations  15 us (2%)
  starting transfers between devices  9.72 us (1%)
    reduce_scatter x1, waiting for transfers between devices, sum_together(): lax.psum_scatter(lines, axis, tiled=True).reshape(-1)  188 us
    psum x1, waiting for transfers between devices, on_device(): lax.psum(down_part, 'tensor')  109 us
    psum x1, waiting for transfers between devices, on_device(): grad_norm_two = lax.psum(norm_two_part, 'tensor')  79.5 us
    psum x1, waiting for transfers between devices, on_device(): branch = lax.psum(branch_part, 'tensor')  65.5 us
    all_gather x1, waiting for transfers between devices, rows_first(): result = lax.all_gather(both, axis, axis=0, tiled=True)  40.1 us
    reduce_sum x4, other arithmetic, layer_norm(): return center * lax.rsqrt(spread + NORM_EPS) * (1.0 + offset) + shift  18.1 us
  transfers between devices with their start and end apart: 6, of which 5 were waited for; matrix products, arithmetic and copies ran while one was open for 15% of the time, Pallas kernels for 0%

commit v1 on v0

v1 whole, which is shorter than its diff:
```python
import functools

import jax
import jax.numpy as jnp
from jax import lax
from jax.experimental import pallas as pl
from jax.experimental.pallas import tpu as pltpu
from jax.sharding import PartitionSpec as P

MESH = pl.DeviceIdType.MESH
ORDERS = ((0, 1, 2), (1, 2, 0), (2, 0, 1))


class Place:
    def __init__(self):
        f = lax.axis_index("fsdp")
        t = lax.axis_index("tensor")
        self.x = f % 4
        self.y = f // 8
        self.z = ((f // 4) % 2) * 2 + t // 2
        self.core = t % 2
        self.at = (self.x, self.y, self.z)
        self.step = 1 - 2 * self.core

    def device(self, at=None, core=None):
        x, y, z = self.at if at is None else at
        core = self.core if core is None else core
        return (y * 8 + (z // 2) * 4 + x, (z % 2) * 2 + core)

    def along(self, axis, by):
        at = list(self.at)
        at[axis] = (at[axis] + by + 4) % 4
        return self.device(at)

    def sibling(self):
        return self.device(core=1 - self.core)

    def partners(self):
        ring = [self.along(axis, by) for axis in range(3) for by in (1, 3)]
        other_z = (self.z // 2) * 2 + 1 - self.z % 2
        across = self.device((self.x, self.y, other_z), 1 - self.core)
        return ring + [self.sibling(), across]


def greet(place):
    barrier = pltpu.get_barrier_semaphore()
    partners = place.partners()
    for device in partners:
        pl.semaphore_signal(barrier, inc=1, device_id=device, device_id_type=MESH)
    pl.semaphore_wait(barrier, len(partners))


def block_of(ref, lead, place, core, done, axis=None, shift=0):
    full = slice(None)
    at = list(place.at)
    if axis is not None:
        at[axis] = (at[axis] + shift + 4) % 4
    x, y, z = at
    x = full if 0 in done else x
    y = full if 1 in done else y
    zl, zh = (full, full) if 2 in done else (z % 2, z // 2)
    index = (*lead, zl, core, y, zh, x) if core is not None else (*lead, zl, y, zh, x)
    return ref.at[index]


def gather_kernel(w_ref, s_ref, gw_ref, gs_ref, own_sem, out_sem, in_sem, sib_out, sib_in, small_out, small_in):
    place = Place()
    core, step = place.core, place.step
    t = lax.axis_index("tensor")
    greet(place)
    other_z = (place.z // 2) * 2 + 1 - place.z % 2
    mates = [
        place.sibling(),
        place.device((place.x, place.y, other_z)),
        place.device((place.x, place.y, other_z), 1 - core),
    ]
    small = []
    for k, mate in enumerate(mates):
        copy = pltpu.make_async_remote_copy(s_ref, gs_ref.at[t], small_out.at[k], small_in.at[k], mate, MESH)
        copy.start()
        small.append(copy)
    small_own = pltpu.make_async_copy(s_ref, gs_ref.at[t], own_sem.at[3])
    small_own.start()

    def send(src, dst, slot, outs, ins, device):
        copy = pltpu.make_async_remote_copy(src, dst, outs.at[slot], ins.at[slot], device, MESH)
        copy.start()
        return copy

    waits = []
    own = []
    for p in range(3):
        mine = block_of(gw_ref, (p,), place, core, ())
        copy = pltpu.make_async_copy(w_ref.at[p], mine, own_sem.at[p])
        copy.start()
        own.append(copy)
    for p in range(3):
        own[p].wait()
        mine = block_of(gw_ref, (p,), place, core, ())
        waits.append(send(mine, mine, (p, 3, 0), sib_out, sib_in, place.sibling()))
    for phase in range(3):
        for p in range(3):
            axis, done = ORDERS[p][phase], ORDERS[p][:phase]
            mine = block_of(gw_ref, (p,), place, core, done)
            waits.append(send(mine, mine, (p, phase, 0), out_sem, in_sem, place.along(axis, step)))
            waits.append(send(mine, mine, (p, phase, 1), out_sem, in_sem, place.along(axis, -step)))
        def arrived(p, phase, kind, shift):
            axis, done = ORDERS[p][phase], ORDERS[p][:phase]
            block = block_of(gw_ref, (p,), place, core, done, axis, shift)
            pltpu.make_async_remote_copy(
                block, block, out_sem.at[p, phase, kind], in_sem.at[p, phase, kind], place.sibling(), MESH
            ).wait_recv()
            return block
        for p in range(3):
            axis = ORDERS[p][phase]
            block = arrived(p, phase, 0, -step)
            waits.append(send(block, block, (p, phase, 2), out_sem, in_sem, place.along(axis, step)))
            waits.append(send(block, block, (p, phase, 0), sib_out, sib_in, place.sibling()))
        for p in range(3):
            block = arrived(p, phase, 1, step)
            waits.append(send(block, block, (p, phase, 1), sib_out, sib_in, place.sibling()))
        for p in range(3):
            block = arrived(p, phase, 2, 2)
            waits.append(send(block, block, (p, phase, 2), sib_out, sib_in, place.sibling()))
    for p in range(3):
        block = block_of(gw_ref, (p,), place, 1 - core, ())
        pltpu.make_async_remote_copy(block, block, sib_out.at[p, 3, 0], sib_in.at[p, 3, 0], place.sibling(), MESH).wait_recv()
        for phase in range(3):
            axis, done = ORDERS[p][phase], ORDERS[p][:phase]
            for kind, shift in enumerate((step, -step, 2)):
                block = block_of(gw_ref, (p,), place, 1 - core, done, axis, shift)
                pltpu.make_async_remote_copy(
                    block, block, sib_out.at[p, phase, kind], sib_in.at[p, phase, kind], place.sibling(), MESH
                ).wait_recv()
    for copy in waits:
        copy.wait_send()
    small_own.wait()
    for copy in small:
        copy.wait()


def gather(w, s):
    return pl.pallas_call(
        gather_kernel,
        out_shape=(
            jax.ShapeDtypeStruct((3, 2, 2, 4, 2, 4, 16, 512), jnp.bfloat16),
            jax.ShapeDtypeStruct((4, 16, 128), jnp.float32),
        ),
        in_specs=[pl.BlockSpec(memory_space=pl.ANY)] * 2,
        out_specs=[pl.BlockSpec(memory_space=pl.ANY)] * 2,
        scratch_shapes=[
            pltpu.SemaphoreType.DMA((4,)),
            pltpu.SemaphoreType.DMA((3, 3, 3)),
            pltpu.SemaphoreType.DMA((3, 3, 3)),
            pltpu.SemaphoreType.DMA((3, 4, 3)),
            pltpu.SemaphoreType.DMA((3, 4, 3)),
            pltpu.SemaphoreType.DMA((3,)),
            pltpu.SemaphoreType.DMA((3,)),
        ],
        compiler_params=pltpu.CompilerParams(collective_id=0, has_side_effects=True),
        name="gather_weights",
    )(w, s)


LOW = jnp.bfloat16
FULL = jnp.float32
EPS = 1e-5
SCALE = 32.0 ** -0.5
BLOCKED = -1e30


def mm(a, b):
    return lax.dot_general(a, b, (((1,), (0,)), ((), ())), preferred_element_type=FULL)


def mm_nt(a, b):
    return lax.dot_general(a, b, (((1,), (1,)), ((), ())), preferred_element_type=FULL)


def mm_tn(a, b):
    return lax.dot_general(a, b, (((0,), (0,)), ((), ())), preferred_element_type=FULL)


def three_lows(a):
    high = a.astype(LOW)
    rest = a - high.astype(FULL)
    middle = rest.astype(LOW)
    last = (rest - middle.astype(FULL)).astype(LOW)
    return jnp.concatenate([high, middle, last], axis=0)


def normed(v):
    center = v - jnp.mean(v, axis=-1, keepdims=True)
    r = lax.rsqrt(jnp.mean(center * center, axis=-1, keepdims=True) + EPS)
    return center * r, r


def norm_back(n, x, r, offset):
    q = n * (1.0 + offset)
    return r * (q - jnp.mean(q, axis=-1, keepdims=True) - x * jnp.mean(q * x, axis=-1, keepdims=True))


def gelu_parts(u):
    size = jnp.abs(u)
    k = 1.0 / (1.0 + (0.3275911 * 0.7071067811865476) * size)
    bell = jnp.exp(-0.5 * u * u)
    poly = k * (0.254829592 + k * (-0.284496736 + k * (1.421413741 + k * (-1.453152027 + k * 1.061405429))))
    tail = 0.5 * poly * bell
    share = jnp.where(u < 0, tail, 1.0 - tail)
    return u * share, share + u * bell * 0.3989422804014327


def lane_mask(h):
    lane = lax.broadcasted_iota(jnp.int32, (128, 128), 1)
    return (lane >= h * 32) & (lane < h * 32 + 32)


def keep(mask, a):
    return jnp.where(mask, a, jnp.zeros_like(a))


def middle_kernel(
    images, cotangents, gw, gs, vec, idx,
    grads, block, igrad, small,
    img_in, cot_in, w, tok, cot, cot_low, cot_t, n1, n1_t, x1, r1, n2, n2_t, x2, r2,
    qkv, probs, att, mid, hid, gpre, gmid, gml, gml_t, dqkv, onehot, spread, bias, dsum, table, field, sems,
    mine,
):
    first = mine()
    in_copies = [
        pltpu.make_async_copy(images.at[pl.ds(first, 2)], img_in, sems.at[0]),
        pltpu.make_async_copy(cotangents.at[pl.ds(first, 2)], cot_in, sems.at[1]),
    ]
    w_copies = [pltpu.make_async_copy(gw.at[p], w.at[p], sems.at[2 + p]) for p in range(3)]
    for copy in in_copies + w_copies:
        copy.start()
    small[...] = jnp.zeros((16, 768), FULL)
    tok[...] = jnp.zeros((512, 512), FULL)
    cot[...] = jnp.zeros((512, 512), FULL)
    for t in range(4):
        table[t * 4 : t * 4 + 4, 0:128] = gs[t, 0:4, :]
        table[t * 4 : t * 4 + 4, 128:256] = gs[t, 4:8, :]
    row_id = lax.broadcasted_iota(jnp.int32, (256, 128), 0)
    for i in range(49):
        onehot[:, i * 128 : (i + 1) * 128] = (row_id == idx[i : i + 1, :]).astype(FULL).astype(LOW)
    parts = three_lows(table[...])
    spread[...] = mm(parts, onehot[...])
    lane = lax.broadcasted_iota(jnp.int32, (16, 128), 1)
    low_side = lane < 49
    high_side = (lane >= 64) & (lane < 113)
    for i in range(64):
        if i < 49:
            at = slice(i * 128, (i + 1) * 128)
            line = spread[0:16, at] + spread[16:32, at] + spread[32:48, at]
        else:
            line = jnp.zeros((16, 128), FULL)
        bias[i * 16 : (i + 1) * 16, :] = jnp.where(low_side, line, BLOCKED)
        bias[(64 + i) * 16 : (65 + i) * 16, :] = jnp.where(high_side, line, BLOCKED)
    for copy in in_copies:
        copy.wait()

    for i in range(28):
        image, r = i // 14, i % 14
        top = (image * 4 + (r // 7) * 2) * 64 + (r % 7) * 7
        for side, (src, dst) in enumerate(((img_in, tok), (cot_in, cot))):
            page = field.at[(2 * i + side) % 4]
            page[0:14, :] = src[image, r].astype(FULL)
            dst[top : top + 7, :] = page[0:7, :]
            dst[top + 64 : top + 71, :] = page[7:14, :]

    def start(k, _):
        rows = pl.ds(pl.multiple_of(k * 64, 64), 64)
        x, r = normed(tok[rows, :])
        x1[rows, :] = x
        r1[rows, :] = r
        n1[rows, :] = (x * (1.0 + vec[0:1, :]) + vec[1:2, :]).astype(LOW)
        c = cot[rows, :]
        cot_low[rows, :] = c.astype(LOW)
        small[5:6, 0:512] += jnp.sum(c, axis=0, keepdims=True)
        return 0

    lax.fori_loop(0, 8, start, 0)
    n1_t[...] = n1[...].T
    cot_t[...] = cot_low[...].T
    w_copies[0].wait()

    def forward(t, _):
        mixed = mm(n1[...], w[0, t, :, 0:384])
        q_bias, v_bias = gs[t, 8:9, :], gs[t, 9:10, :]
        qkv[t, 0] = (mixed[:, 0:128] + q_bias).astype(LOW)
        qkv[t, 1] = mixed[:, 128:256].astype(LOW)
        qkv[t, 2] = (mixed[:, 256:384] + v_bias).astype(LOW)
        for wp in range(4):
            rows = slice(wp * 128, (wp + 1) * 128)
            q, k, v = qkv[t, 0, rows], qkv[t, 1, rows], qkv[t, 2, rows]
            ps, vs = [], []
            for h in range(4):
                mask = lane_mask(h)
                s = mm_nt(keep(mask, q), k) * SCALE + bias[pl.ds(t * 4 + h, 128, stride=16), :]
                e = jnp.exp(s - jnp.max(s, axis=-1, keepdims=True))
                p = (e / jnp.sum(e, axis=-1, keepdims=True)).astype(LOW)
                probs[t, wp, h] = p
                ps.append(p)
                vs.append(keep(mask, v))
            att[t, rows] = mm(jnp.concatenate(ps, axis=1), jnp.concatenate(vs, axis=0)).astype(LOW)
        return 0

    lax.fori_loop(0, 4, forward, 0)

    def second(k, _):
        rows = pl.ds(pl.multiple_of(k * 128, 128), 128)
        acc = tok[rows, :] + vec[2:3, :]
        for t in range(4):
            acc = acc + mm_nt(att[t, rows, :], w[0, t, :, 384:512])
        mid[rows, :] = acc
        x, r = normed(acc)
        x2[rows, :] = x
        r2[rows, :] = r
        n2[rows, :] = (x * (1.0 + vec[3:4, :]) + vec[4:5, :]).astype(LOW)
        return 0

    lax.fori_loop(0, 4, second, 0)
    n2_t[...] = n2[...].T
    w_copies[1].wait()
    w_copies[2].wait()

    def feed(t, _):
        unit = jnp.concatenate([gs[t, 10 + k : 11 + k, :] for k in range(4)], axis=1)

        def rows_of(k, total):
            rows = pl.ds(pl.multiple_of(k * 128, 128), 128)
            pre = mm(n2[rows, :], w[1, t]) + unit
            value, slope = gelu_parts(pre)
            hid[t, rows, :] = value.astype(LOW)
            g = mm(cot_low[rows, :], w[2, t]) * slope
            gpre[t, rows, :] = g.astype(LOW)
            return total + jnp.sum(g, axis=0, keepdims=True)

        small[pl.ds(8 + t, 1), 0:512] = lax.fori_loop(0, 4, rows_of, jnp.zeros((1, 512), FULL))
        grads[1, t] = mm(n2_t[...], gpre[t]).astype(LOW)
        grads[2, t] = mm(cot_t[...], hid[t]).astype(LOW)
        return 0

    lax.fori_loop(0, 4, feed, 0)

    def third(k, _):
        rows = pl.ds(pl.multiple_of(k * 128, 128), 128)
        out = mid[rows, :] + vec[5:6, :]
        n = jnp.zeros((128, 512), FULL)
        for t in range(4):
            out = out + mm_nt(hid[t, rows, :], w[2, t])
            n = n + mm_nt(gpre[t, rows, :], w[1, t])
        mid[rows, :] = out
        x = x2[rows, :]
        g = cot[rows, :] + norm_back(n, x, r2[rows, :], vec[3:4, :])
        gmid[rows, :] = g
        gml[rows, :] = g.astype(LOW)
        small[2:3, 0:512] += jnp.sum(g, axis=0, keepdims=True)
        small[3:4, 0:512] += jnp.sum(n * x, axis=0, keepdims=True)
        small[4:5, 0:512] += jnp.sum(n, axis=0, keepdims=True)
        return 0

    lax.fori_loop(0, 4, third, 0)
    gml_t[...] = gml[...].T

    def backward(t, _):
        ga = mm(gml[...], w[0, t, :, 384:512]).astype(LOW)
        grads[0, t, :, 384:512] = mm(gml_t[...], att[t]).astype(LOW)
        sums = [jnp.zeros((128, 128), FULL) for _ in range(4)]
        sum_q = jnp.zeros((1, 128), FULL)
        sum_v = jnp.zeros((1, 128), FULL)
        for wp in range(4):
            rows = slice(wp * 128, (wp + 1) * 128)
            q, k, v, g = qkv[t, 0, rows], qkv[t, 1, rows], qkv[t, 2, rows], ga[rows]
            dss, ps, ks, qs, gg = [], [], [], [], []
            for h in range(4):
                mask = lane_mask(h)
                p_low = probs[t, wp, h]
                p = p_low.astype(FULL)
                gh = keep(mask, g)
                dp = mm_nt(gh, v)
                ds = (p * (dp - jnp.sum(dp * p, axis=-1, keepdims=True))).astype(LOW)
                sums[h] = sums[h] + ds.astype(FULL)
                dss.append(ds)
                ps.append(p_low)
                ks.append(keep(mask, k))
                qs.append(keep(mask, q))
                gg.append(gh)
            dq = (mm(jnp.concatenate(dss, axis=1), jnp.concatenate(ks, axis=0)) * SCALE).astype(LOW)
            dk = (mm_tn(jnp.concatenate(dss, axis=0), jnp.concatenate(qs, axis=0)) * SCALE).astype(LOW)
            dv = mm_tn(jnp.concatenate(ps, axis=0), jnp.concatenate(gg, axis=0)).astype(LOW)
            dqkv[t, rows, 0:128] = dq
            dqkv[t, rows, 128:256] = dk
            dqkv[t, rows, 256:384] = dv
            sum_q = sum_q + jnp.sum(dq.astype(FULL), axis=0, keepdims=True)
            sum_v = sum_v + jnp.sum(dv.astype(FULL), axis=0, keepdims=True)
        for h in range(4):
            dsum[pl.ds(t * 4 + h, 128, stride=16), :] = sums[h]
        at = pl.ds(pl.multiple_of(t * 128, 128), 128)
        small[6:7, at] = sum_q
        small[7:8, at] = sum_v
        grads[0, t, :, 0:384] = mm(n1_t[...], dqkv[t]).astype(LOW)
        return 0

    lax.fori_loop(0, 4, backward, 0)

    def last(k, _):
        rows = pl.ds(pl.multiple_of(k * 128, 128), 128)
        n = jnp.zeros((128, 512), FULL)
        for t in range(4):
            n = n + mm_nt(dqkv[t, rows, :], w[0, t, :, 0:384])
        x = x1[rows, :]
        gmid[rows, :] += norm_back(n, x, r1[rows, :], vec[0:1, :])
        small[0:1, 0:512] += jnp.sum(n * x, axis=0, keepdims=True)
        small[1:2, 0:512] += jnp.sum(n, axis=0, keepdims=True)
        return 0

    lax.fori_loop(0, 4, last, 0)
    lines = []
    for i in range(49):
        lines.append(three_lows(dsum[i * 16 : (i + 1) * 16, :] + dsum[(64 + i) * 16 : (65 + i) * 16, :]))
    total = mm_nt(jnp.concatenate(lines, axis=1), onehot[...])
    small[:, 512:768] = total[0:16] + total[16:32] + total[32:48]

    field[...] = jnp.zeros((4, 16, 512), FULL)
    for i in range(28):
        image, r = i // 14, i % 14
        top = (image * 4 + (r // 7) * 2) * 64 + (r % 7) * 7
        for side, (src, dst) in enumerate(((mid, block), (gmid, igrad))):
            page = field.at[(2 * i + side) % 4]
            page[0:7, :] = src[top : top + 7, :]
            page[7:14, :] = src[top + 64 : top + 71, :]
            dst[image, r] = page[...].astype(LOW)


def middle(images, cotangents, gw, gs, vec, idx, mine):
    vm = lambda *shape, dtype=FULL: pltpu.VMEM(shape, dtype)
    whole = pl.BlockSpec(memory_space=pltpu.VMEM)
    anywhere = pl.BlockSpec(memory_space=pl.ANY)
    return pl.pallas_call(
        functools.partial(middle_kernel, mine=mine),
        out_shape=(
            jax.ShapeDtypeStruct((3, 4, 512, 512), LOW),
            jax.ShapeDtypeStruct((2, 14, 16, 512), LOW),
            jax.ShapeDtypeStruct((2, 14, 16, 512), LOW),
            jax.ShapeDtypeStruct((16, 768), FULL),
        ),
        in_specs=[anywhere] * 3 + [whole] * 3,
        out_specs=[whole] * 4,
        scratch_shapes=[
            vm(2, 14, 14, 512, dtype=LOW), vm(2, 14, 14, 512, dtype=LOW), vm(3, 4, 512, 512, dtype=LOW),
            vm(512, 512), vm(512, 512), vm(512, 512, dtype=LOW), vm(512, 512, dtype=LOW),
            vm(512, 512, dtype=LOW), vm(512, 512, dtype=LOW), vm(512, 512), vm(512, 1),
            vm(512, 512, dtype=LOW), vm(512, 512, dtype=LOW), vm(512, 512), vm(512, 1),
            vm(4, 3, 512, 128, dtype=LOW), vm(4, 4, 4, 128, 128, dtype=LOW), vm(4, 512, 128, dtype=LOW),
            vm(512, 512), vm(4, 512, 512, dtype=LOW), vm(4, 512, 512, dtype=LOW),
            vm(512, 512), vm(512, 512, dtype=LOW), vm(512, 512, dtype=LOW), vm(4, 512, 384, dtype=LOW),
            vm(256, 49 * 128, dtype=LOW), vm(48, 49 * 128), vm(2048, 128), vm(2048, 128), vm(16, 256), vm(4, 16, 512),
            pltpu.SemaphoreType.DMA((5,)),
        ],
        compiler_params=pltpu.CompilerParams(vmem_limit_bytes=62 * 2**20),
        name="block_forward_backward",
    )(images, cotangents, gw, gs, vec, idx)


def wide_index(rel_index):
    edge = jnp.pad(rel_index, ((0, 7), (0, 15)), constant_values=-1)
    return jnp.concatenate([edge, edge], axis=1)


def block_dims(full):
    dims = []
    for axis, size in ((2, 2), (1, 4), (2, 2), (0, 4)):
        if axis in full:
            dims.append(size)
    return tuple(dims)


def each(dims, fn):
    outer = dims[:-1]
    count = 1
    for size in outer:
        count *= size
    if count == 1:
        fn(())
        return

    def body(n, _):
        index = []
        for size in reversed(outer):
            index.append(n % size)
            n = n // size
        fn(tuple(reversed(index)))
        return 0

    lax.fori_loop(0, count, body, 0)


def scatter_kernel(
    g_ref, block_ref, igrad_ref, small_ref,
    mine_ref, blocks_ref, igrads_ref, total_ref,
    sib, part, slot00, slot10, slot20, slot01, slot11, slot21, slot02, slot12, slot22, steps,
    local_sem, sib_out, sib_in, out_sem, in_sem, small_out, small_in, mate_out, mate_in,
):
    slots = ((slot00, slot01, slot02), (slot10, slot11, slot12), (slot20, slot21, slot22))
    place = Place()
    core, step = place.core, place.step
    t = lax.axis_index("tensor")
    other_z = (place.z // 2) * 2 + 1 - place.z % 2
    sibling = place.sibling()
    z_mate = place.device((place.x, place.y, other_z))
    across = place.device((place.x, place.y, other_z), 1 - core)
    barrier = pltpu.get_barrier_semaphore()
    partners = [place.along(axis, by) for axis in range(3) for by in (1, 2, 3)] + [sibling, across]
    for device in partners:
        pl.semaphore_signal(barrier, inc=1, device_id=device, device_id_type=MESH)
    pl.semaphore_wait(barrier, len(partners))

    sends = []

    def send(src, dst, out, into, device):
        copy = pltpu.make_async_remote_copy(src, dst, out, into, device, MESH)
        copy.start()
        sends.append(copy)

    def wait_in(block, out, into):
        pltpu.make_async_remote_copy(block, block, out, into, sibling, MESH).wait_recv()

    shifts = (2, -step, step, 0)
    for k in range(4):
        for p in range(3):
            axis = ORDERS[p][2]
            full = ORDERS[p][:2]
            shift = (2, step, -step, 0)[k]
            src = block_of(g_ref, (p,), place, 1 - core, full, axis, shift)
            dst = block_of(sib, (p,), place, None, full, axis, shift)
            send(src, dst, sib_out.at[p, k], sib_in.at[p, k], sibling)
    own = []
    for p in range(3):
        copy = pltpu.make_async_copy(g_ref.at[p, :, core], part.at[p], local_sem.at[p])
        copy.start()
        own.append(copy)
    outs = ((block_ref, blocks_ref), (igrad_ref, igrads_ref))
    rows = pl.ds(t * 2, 2)
    for n, (src, dst) in enumerate(outs):
        copy = pltpu.make_async_copy(src, dst.at[rows], local_sem.at[3 + n])
        copy.start()
        own.append(copy)
        send(src, dst.at[rows], mate_out.at[n, 0], mate_in.at[n, 0], z_mate)
        send(src, dst.at[rows], mate_out.at[n, 1], mate_in.at[n, 1], sibling)

    def small_start(k):
        if k < 3:
            at = place.at[k]
            for shift in (1, 2, 3):
                send(
                    steps.at[k, at], steps.at[k, at], small_out.at[k, shift - 1], small_in.at[k, shift - 1],
                    place.along(k, shift),
                )
        else:
            send(steps.at[3, core], steps.at[3, core], small_out.at[3, 0], small_in.at[3, 0], sibling)

    def small_finish(k):
        if k < 3:
            for shift in (1, 2, 3):
                at = (place.at[k] - shift + 4) % 4
                wait_in(steps.at[k, at], small_out.at[k, shift - 1], small_in.at[k, shift - 1])
            return (steps[k, 0] + steps[k, 1]) + (steps[k, 2] + steps[k, 3])
        wait_in(steps.at[3, 1 - core], small_out.at[3, 0], small_in.at[3, 0])
        return steps[3, 0] + steps[3, 1]

    def small_next(k):
        value = small_finish(k)
        steps[k + 1, place.at[k + 1] if k < 2 else core] = value
        small_start(k + 1)

    steps[0, place.x] = small_ref[...]
    small_start(0)
    for p in range(3):
        own[p].wait()

    def add_sibling(p, k):
        axis, full = ORDERS[p][2], ORDERS[p][:2]
        there = block_of(sib, (p,), place, None, full, axis, shifts[k])
        here = block_of(part, (p,), place, None, full, axis, shifts[k])
        wait_in(there, sib_out.at[p, k], sib_in.at[p, k])

        def add(index):
            here[index] = here[index] + there[index]

        each(block_dims(full), add)

    def wait_slot(p, phase, kind):
        slot = slots[p][phase].at[kind]
        wait_in(slot, out_sem.at[p, phase, kind], in_sem.at[p, phase, kind])
        return slot

    for phase in range(3):
        rank = 2 - phase
        for k, shift, kind, toward in ((0, 2, 0, step), (1, -step, 2, -step)):
            for p in range(3):
                axis, full = ORDERS[p][rank], ORDERS[p][:rank]
                if phase == 0:
                    add_sibling(p, k)
                send(
                    block_of(part, (p,), place, None, full, axis, shift), slots[p][phase].at[kind],
                    out_sem.at[p, phase, kind], in_sem.at[p, phase, kind], place.along(axis, toward),
                )
        if phase == 0:
            for p in range(3):
                add_sibling(p, 2)
            small_next(0)
        if phase == 1:
            small_next(2)
        for p in range(3):
            axis, full = ORDERS[p][rank], ORDERS[p][:rank]
            slot = wait_slot(p, phase, 0)
            near = block_of(part, (p,), place, None, full, axis, step)

            def add(index):
                near[index] = near[index] + slot[index]

            each(block_dims(full) or (1,), add)
            send(
                near, slots[p][phase].at[1],
                out_sem.at[p, phase, 1], in_sem.at[p, phase, 1], place.along(axis, step),
            )
        if phase == 0:
            for p in range(3):
                add_sibling(p, 3)
            small_next(1)
        for p in range(3):
            axis, full = ORDERS[p][rank], ORDERS[p][:rank]
            one = wait_slot(p, phase, 2)
            two = wait_slot(p, phase, 1)
            here = block_of(part, (p,), place, None, full, axis, 0)
            if phase == 2:
                mine_ref[p] = here[...].astype(FULL) + one[...].astype(FULL) + two[...].astype(FULL)
            else:
                def add_both(index):
                    total = here[index].astype(FULL) + one[index].astype(FULL) + two[index].astype(FULL)
                    here[index] = total.astype(LOW)

                each(block_dims(full), add_both)
    total_ref[...] = small_finish(3)
    mate = place.z % 2
    their = pl.ds(((1 - mate) * 2 + core) * 2, 2)
    for n, (src, dst) in enumerate(outs):
        wait_in(dst.at[their], mate_out.at[n, 0], mate_in.at[n, 0])
        send(dst.at[their], dst.at[their], mate_out.at[n, 2], mate_in.at[n, 2], sibling)
    for n, (src, dst) in enumerate(outs):
        wait_in(dst.at[pl.ds((mate * 2 + 1 - core) * 2, 2)], mate_out.at[n, 1], mate_in.at[n, 1])
        wait_in(dst.at[pl.ds(((1 - mate) * 2 + 1 - core) * 2, 2)], mate_out.at[n, 2], mate_in.at[n, 2])
    for copy in own[3:]:
        copy.wait()
    for copy in sends:
        copy.wait_send()


def scatter(g, block, igrad, small):
    anywhere = pl.BlockSpec(memory_space=pl.ANY)
    whole = pl.BlockSpec(memory_space=pltpu.VMEM)
    slot_shapes = [
        pltpu.VMEM((3, *block_dims(ORDERS[p][: 2 - phase]), 16, 512), LOW) for phase in range(3) for p in range(3)
    ]
    return pl.pallas_call(
        scatter_kernel,
        out_shape=(
            jax.ShapeDtypeStruct((3, 16, 512), FULL),
            jax.ShapeDtypeStruct((8, 14, 16, 512), LOW),
            jax.ShapeDtypeStruct((8, 14, 16, 512), LOW),
            jax.ShapeDtypeStruct((16, 768), FULL),
        ),
        in_specs=[anywhere, anywhere, anywhere, whole],
        out_specs=[whole, anywhere, anywhere, whole],
        scratch_shapes=[
            pltpu.VMEM((3, 2, 4, 2, 4, 16, 512), LOW),
            pltpu.VMEM((3, 2, 4, 2, 4, 16, 512), LOW),
            *slot_shapes,
            pltpu.VMEM((4, 4, 16, 768), FULL),
            pltpu.SemaphoreType.DMA((5,)),
            pltpu.SemaphoreType.DMA((3, 4)),
            pltpu.SemaphoreType.DMA((3, 4)),
            pltpu.SemaphoreType.DMA((3, 3, 3)),
            pltpu.SemaphoreType.DMA((3, 3, 3)),
            pltpu.SemaphoreType.DMA((4, 3)),
            pltpu.SemaphoreType.DMA((4, 3)),
            pltpu.SemaphoreType.DMA((2, 3)),
            pltpu.SemaphoreType.DMA((2, 3)),
        ],
        compiler_params=pltpu.CompilerParams(
            collective_id=1, has_side_effects=True, vmem_limit_bytes=40 * 2**20
        ),
        name="scatter_gradients",
    )(g, block, igrad, small)


STEP = 10
REL = 169
BETA_ONE = 0.9
BETA_TWO = 0.999
ADAM_EPS = 1e-08
RATE_MATRIX = 0.1
RATE_VECTOR = 0.2
RATE_TABLE = 0.5
WEIGHT_DECAY = 0.05


def adam_step(weight, grad, first, second, rate, decay):
    first_new = BETA_ONE * first + (1.0 - BETA_ONE) * grad
    second_new = BETA_TWO * second + (1.0 - BETA_TWO) * grad * grad
    first_hat = first_new / (1.0 - BETA_ONE**STEP)
    second_hat = second_new / (1.0 - BETA_TWO**STEP)
    updated = weight - rate * (first_hat / (jnp.sqrt(second_hat) + ADAM_EPS) + decay * weight)
    return (updated, first_new, second_new)


def on_device(
    images,
    out_grad,
    rel_index,
    attn_weight,
    attn_first,
    attn_second,
    proj_weight,
    proj_first,
    proj_second,
    up_weight,
    up_first,
    up_second,
    down_weight,
    down_first,
    down_second,
    vectors,
    vec_first,
    vec_second,
    head_bias,
    head_first,
    head_second,
    unit_bias,
    unit_first,
    unit_second,
    rel_table,
    table_first,
    table_second,
):
    t = lax.axis_index("tensor")
    shards = jnp.stack(
        [
            jnp.concatenate([attn_weight.reshape(16, 384), proj_weight.T], axis=1),
            up_weight,
            down_weight.T,
        ]
    ).astype(LOW)
    lines = jnp.pad(rel_table.T, ((0, 0), (0, 256 - REL)))
    small_in = jnp.concatenate(
        [lines[:, :128], lines[:, 128:], head_bias, unit_bias.reshape(4, 128), jnp.zeros((2, 128), FULL)], axis=0
    )
    weights, smalls = gather(shards, small_in)
    grads, block, igrad, small = middle(
        images, out_grad, weights.reshape(3, 4, 512, 512), smalls, vectors, wide_index(rel_index),
        lambda: lax.axis_index("tensor") * 2,
    )
    mine, blocks, igrads, total = scatter(grads.reshape(3, 2, 2, 4, 2, 4, 16, 512), block, igrad, small)
    block_out = blocks[:, :, :14]
    images_grad = igrads[:, :, :14].astype(FULL)
    vec_grad = total[0:6, :512]
    head_grad = lax.dynamic_slice(total, (6, t * 128), (2, 128))
    unit_grad = lax.dynamic_slice(total, (8 + t, 0), (1, 512)).reshape(512)
    table_grad = lax.dynamic_slice(total, (t * 4, 512), (4, REL)).T
    attn_grad = mine[0, :, :384].reshape(16, 3, 128)
    proj_grad = mine[0, :, 384:].T
    up_grad = mine[1]
    down_grad = mine[2].T
    attn_out = adam_step(attn_weight, attn_grad, attn_first, attn_second, RATE_MATRIX, WEIGHT_DECAY)
    proj_out = adam_step(proj_weight, proj_grad, proj_first, proj_second, RATE_MATRIX, WEIGHT_DECAY)
    up_out = adam_step(up_weight, up_grad, up_first, up_second, RATE_MATRIX, WEIGHT_DECAY)
    down_out = adam_step(down_weight, down_grad, down_first, down_second, RATE_MATRIX, WEIGHT_DECAY)
    vec_out = adam_step(vectors, vec_grad, vec_first, vec_second, RATE_VECTOR, 0.0)
    head_out = adam_step(head_bias, head_grad, head_first, head_second, RATE_VECTOR, 0.0)
    unit_out = adam_step(unit_bias, unit_grad, unit_first, unit_second, RATE_VECTOR, 0.0)
    table_out = adam_step(rel_table, table_grad, table_first, table_second, RATE_TABLE, 0.0)
    return (
        (block_out, images_grad)
        + attn_out
        + proj_out
        + up_out
        + down_out
        + vec_out
        + head_out
        + unit_out
        + table_out
    )


def solution(mesh):
    in_specs = (
        P("fsdp", None, None, None),
        P("fsdp", None, None, None),
        P(),
        P("fsdp", None, "tensor"),
        P("fsdp", None, "tensor"),
        P("fsdp", None, "tensor"),
        P("tensor", "fsdp"),
        P("tensor", "fsdp"),
        P("tensor", "fsdp"),
        P("fsdp", "tensor"),
        P("fsdp", "tensor"),
        P("fsdp", "tensor"),
        P("tensor", "fsdp"),
        P("tensor", "fsdp"),
        P("tensor", "fsdp"),
        P(),
        P(),
        P(),
        P(None, "tensor"),
        P(None, "tensor"),
        P(None, "tensor"),
        P("tensor"),
        P("tensor"),
        P("tensor"),
        P(None, "tensor"),
        P(None, "tensor"),
        P(None, "tensor"),
    )
    out_specs = (
        P("fsdp", None, None, None),
        P("fsdp", None, None, None),
        P("fsdp", None, "tensor"),
        P("fsdp", None, "tensor"),
        P("fsdp", None, "tensor"),
        P("tensor", "fsdp"),
        P("tensor", "fsdp"),
        P("tensor", "fsdp"),
        P("fsdp", "tensor"),
        P("fsdp", "tensor"),
        P("fsdp", "tensor"),
        P("tensor", "fsdp"),
        P("tensor", "fsdp"),
        P("tensor", "fsdp"),
        P(),
        P(),
        P(),
        P(None, "tensor"),
        P(None, "tensor"),
        P(None, "tensor"),
        P("tensor"),
        P("tensor"),
        P("tensor"),
        P(None, "tensor"),
        P(None, "tensor"),
        P(None, "tensor"),
    )
    return jax.shard_map(
        on_device, mesh=mesh, in_specs=in_specs, out_specs=out_specs, check_vma=False
    )
```

time: 769 us -> 177 us (0.23)
  waiting for transfers between devices: 482 us -> 0 us
  Pallas kernels: 0 us -> 143 us
  local copies, waits for them, and re-layouts: 113 us -> 20.9 us
  matrix products: 66.6 us -> 0 us
  other arithmetic: 76.7 us -> 11.5 us
  between operations: 15 us -> 0.96 us
  starting transfers between devices: 9.72 us -> 0 us
    psum x3 -> x0, waiting for transfers between devices: 254 us -> none  [the longest x1 109 us: on_device(): lax.psum(down_part, 'tensor')]
    reduce_scatter x1 -> x0, waiting for transfers between devices: 188 us -> none  [sum_together(): lax.psum_scatter(lines, axis, tiled=True).reshape(-1)]
    pallas_call x0 -> x3, Pallas kernels: none -> 143 us  [the longest x1 53.9 us: scatter(): pl.pallas_call(scatter_kernel, out_shape=(jax.ShapeDtypeStruct((3, 16, 51...]
    dot_general x20 -> x0, matrix products: 66.6 us -> none  [the longest x1 8.31 us: on_device(): jnp.einsum('wtf,wtd->fd', hidden_low, cot_low, preferred_element_type=ful...]
    reduce_sum x13 -> x0, other arithmetic: 40.4 us -> none  [the longest x4 18.1 us: layer_norm(): return center * lax.rsqrt(spread + NORM_EPS) * (1.0 + offset) + shift]
    all_gather x1 -> x0, waiting for transfers between devices: 40.1 us -> none  [rows_first(): result = lax.all_gather(both, axis, axis=0, tiled=True)]
    reshape x21 -> x0, local copies, waits for them, and re-layouts: 34.1 us -> none  [the longest x4 14.3 us: from_windows(): field.reshape(count, SIDE // WIN, SIDE // WIN, WIN, WIN, field.shape[-1])]
    dot_general x4 -> x0, local copies, waits for them, and re-layouts: 18.5 us -> none  [the longest x1 8.76 us: on_device(): jnp.einsum('wtf,wtd->fd', hidden_low, cot_low, preferred_element_type=ful...]
  transfers between devices with their start and end apart: 6 -> 0, of which waited for: 5 -> 0; matrix products, arithmetic and copies ran while one was open for 15% -> 0% of each run, Pallas kernels for 0% -> 0%
where the time goes in v1:
time: 177 us; the launch traced here: 176 us
  Pallas kernels  143 us (81%)
  local copies, waits for them, and re-layouts  20.9 us (12%)
  other arithmetic  11.5 us (6%)
    pallas_call x1, Pallas kernels, scatter(): pl.pallas_call(scatter_kernel, out_shape=(jax.ShapeDtypeStruct((3, 16, 51...  53.9 us
    pallas_call x1, Pallas kernels, middle(): pl.pallas_call(functools.partial(middle_kernel, mine=mine), out_shape=(ja...  47 us
    pallas_call x1, Pallas kernels, gather(): pl.pallas_call(gather_kernel, out_shape=(jax.ShapeDtypeStruct((3, 2, 2, 4...  41.7 us
    unnamed x66, local copies, waits for them, and re-layouts  18.2 us
    sub x8, other arithmetic, adam_step(): weight - rate * (first_hat / (jnp.sqrt(second_hat) + ADAM_EPS) + decay *...  5.1 us

profile of v1, /device:TPU:1, one launch (start us, length us, event | category | flops | bytes accessed | tf_op | source)
XLA Modules:
  0.0 176.0 jit_solution(7893341565203839413)
XLA Ops:
  0.7 0.7 pad_slice_fusion
  1.4 1.9 %concatenate.11.s_ref = f32[16,128]{1,0:T(8,128)} concatenate(f32[4,128]{1,0:T(4,128)S(1)} %get-tuple-element.149, f32[4,128]{1,0:T(4,128)S(1)} %get-tuple-element.148, f32[2,128]{1,0:T(2,128)} %param.45, f32[4,128]{1,0:T(4,128)} %bitcast.58, f32[2,128]{1,0:T(2,128)S(1)} %broadcast.35), dimensions={0} | concatenate | bytes 16384 | tf_op jit(solution)/shard_map/concatenate | solution.py:756
  3.3 0.7 copy_bitcast_fusion
  4.0 0.7 convert_bitcast_fusion.3
  4.7 0.8 convert_bitcast_fusion
  5.5 0.9 convert_bitcast_fusion.1
  6.4 0.6 pad_maximum_fusion.w_ref
  7.0 41.7 %gather_weights.1 = (bf16[3,2,2,4,2,4,16,512]{7,6,5,4,3,2,1,0:T(8,128)(2,1)}, f32[4,16,128]{2,1,0:T(8,128)}) custom-call(bf16[3,16,512]{2,1,0:T(8,128)(2,1)} %pad_maximum_fusion.w_ref, f32[16,128]{1,0:T(8,128)} %concatenate.11.s_ref), custom_call_target="tpu_custom_call" | custom-call | tf_op jit(solution)/shard_map/gather_weights/pallas_call | solution.py:143
  48.8 3.2 %copy.74.images = bf16[8,14,14,512]{3,2,1,0:T(8,128)(2,1)} copy(bf16[8,14,14,512]{3,0,2,1:T(8,128)(2,1)} %param.27) | data formatting | bytes 3211264 | tf_op args[0]
  52.0 0.0 copy-done.5
  52.0 1.8 %copy.75.cotangents = bf16[8,14,14,512]{3,2,1,0:T(8,128)(2,1)} copy(bf16[8,14,14,512]{3,0,2,1:T(8,128)(2,1)S(1)} %copy-done.5) | data formatting | bytes 3211264 | tf_op args[1]
  53.7 0.0 copy-done.15
  53.8 0.7 pad_add_fusion.idx
  54.4 47.0 %block_forward_backward.1 = (bf16[3,4,512,512]{3,2,1,0:T(8,128)(2,1)}, bf16[2,14,16,512]{3,2,1,0:T(8,128)(2,1)}, bf16[2,14,16,512]{3,2,1,0:T(8,128)(2,1)}, f32[16,768]{1,0:T(8,128)}) custom-call(bf16[8,14,14,512]{3,2,1,0:T(8,128)(2,1)} %copy.74.images, bf16[8,14,14,512]{3,2,1,0:T(8,128)(2,1)} %copy.75.cotangents, bf16[3,4,512,512]{3,2,1,0:T(8,128)(2,1)} %bitcast.55, ...), custom_call_target="tpu_custom_call" | custom-call | tf_op jit(solution)/shard_map/block_forward_backward/pallas_call | solution.py:440
  101.5 0.0 copy-start
  101.5 2.8 %copy-done = bf16[3,4,512,512]{3,2,1,0:T(8,128)(2,1)S(1)} copy-done((bf16[3,4,512,512]{3,2,1,0:T(8,128)(2,1)S(1)}, bf16[3,4,512,512]{3,2,1,0:T(8,128)(2,1)}, u32[]{:S(2)}) %copy-start) | copy-done | bytes 6291480
  104.3 1.0 copy-done.2
  105.3 1.0 copy-done.3
  106.3 0.8 copy-done.4
  107.1 0.0 copy-start.29
  107.1 0.0 copy-start.30
  107.1 0.0 copy-start.23
  107.2 0.0 copy-start.27
  107.2 0.0 copy-start.28
  107.2 0.0 copy-start.8
  107.2 0.0 copy-start.17
  107.2 0.0 copy-start.18
  107.2 0.0 copy-start.6
  107.2 0.0 copy-start.10
  107.2 0.0 copy-start.11
  107.3 0.0 copy-start.7
  107.3 0.0 copy-start.12
  107.3 0.0 copy-start.13
  107.3 0.0 copy-start.9
  107.3 0.0 copy-start.19
  107.3 0.0 copy-start.20
  107.3 0.0 copy-start.14
  107.3 0.0 copy-start.21
  107.4 0.0 copy-start.22
  107.4 53.9 %scatter_gradients.1 = (f32[3,16,512]{2,1,0:T(8,128)S(1)}, bf16[8,14,16,512]{3,2,1,0:T(8,128)(2,1)S(1)}, bf16[8,14,16,512]{3,2,1,0:T(8,128)(2,1)S(1)}, f32[16,768]{1,0:T(8,128)S(1)}) custom-call(bf16[3,2,2,4,2,4,16,512]{7,6,5,4,3,2,1,0:T(8,128)(2,1)S(1)} %bitcast.53, bf16[2,14,16,512]{3,2,1,0:T(8,128)(2,1)S(1)} %copy-done.2, ...), custom_call_target="tpu_custom_call" | custom-call | tf_op jit(solution)/shard_map/scatter_gradients/pallas_call | solution.py:666
  161.3 0.0 copy-start.1
  161.3 1.2 copy-done.1
  162.5 0.0 copy-done.16
  162.5 0.0 copy-done.24
  162.5 0.0 copy-done.25
  162.5 0.6 multiply_subtract_fusion.5
  163.1 0.0 copy-done.26
  163.1 0.0 copy-done.29
  163.1 0.0 copy-done.30
  163.1 0.7 multiply_subtract_fusion.7
  163.8 0.6 multiply_subtract_fusion.6
  164.5 0.6 multiply_subtract_fusion.2
  165.1 0.0 copy-done.6
  165.1 0.0 copy-done.11
  165.2 0.7 multiply_subtract_fusion
  165.8 0.0 copy-done.13
  165.8 0.7 multiply_subtract_fusion.1
  166.5 0.0 copy-done.19
  166.5 0.6 multiply_subtract_fusion.3
  167.1 0.0 copy-done.21
  167.1 0.6 multiply_subtract_fusion.4
  167.8 2.0 %slice_convert_fusion = f32[8,14,14,512]{3,2,1,0:T(8,128)S(1)} fusion(bf16[8,14,16,512]{3,2,1,0:T(8,128)(2,1)} %copy-done.1), kind=kLoop, calls=%fused_computation | loop fusion | flops 802816 | bytes 4816896 | tf_op jit(solution)/shard_map/convert_element_type | solution.py:766
  169.8 4.1 %copy.80 = f32[8,14,14,512]{3,0,2,1:T(8,128)} copy(f32[8,14,14,512]{3,2,1,0:T(8,128)S(1)} %slice_convert_fusion) | data formatting | bytes 6422528
  173.8 2.2 %copy.79 = bf16[8,14,14,512]{3,0,2,1:T(8,128)(2,1)} copy(bf16[8,14,14,512]{3,2,1,0:T(8,128)(2,1)S(1)} %bitcast.54) | data formatting | bytes 3211264
  (28 shorter events, 0.1 us)
Async XLA Ops:
  5.5 46.5 %copy-start.5 = (bf16[8,14,14,512]{3,0,2,1:T(8,128)(2,1)S(1)}, bf16[8,14,14,512]{3,0,2,1:T(8,128)(2,1)}, u32[]{:S(2)}) copy-start(bf16[8,14,14,512]{3,0,2,1:T(8,128)(2,1)} %param.28) | copy-start | bytes 4816900
  52.0 1.8 %copy-start.15 = (s32[49,49]{1,0:T(8,128)S(1)}, s32[49,49]{1,0:T(8,128)}, u32[]{:S(2)}) copy-start(s32[49,49]{1,0:T(8,128)} %param.29) | copy-start | bytes 28816
  101.5 2.8 %copy-start = (bf16[3,4,512,512]{3,2,1,0:T(8,128)(2,1)S(1)}, bf16[3,4,512,512]{3,2,1,0:T(8,128)(2,1)}, u32[]{:S(2)}) copy-start(bf16[3,4,512,512]{3,2,1,0:T(8,128)(2,1)} %get-tuple-element.38) | copy-start | bytes 18874372
  104.3 1.0 copy-start.2
  105.3 1.0 copy-start.3
  106.3 0.8 copy-start.4
  107.1 55.4 %copy-start.16 = (f32[169,4]{0,1:T(4,128)S(1)}, f32[169,4]{0,1:T(4,128)}, u32[]{:S(2)}) copy-start(f32[169,4]{0,1:T(4,128)} %param.51) | copy-start | bytes 8116
  107.1 55.4 %copy-start.24 = (f32[169,4]{0,1:T(4,128)S(1)}, f32[169,4]{0,1:T(4,128)}, u32[]{:S(2)}) copy-start(f32[169,4]{0,1:T(4,128)} %param.52) | copy-start | bytes 8116
  107.1 55.4 %copy-start.25 = (f32[169,4]{0,1:T(4,128)S(1)}, f32[169,4]{0,1:T(4,128)}, u32[]{:S(2)}) copy-start(f32[169,4]{0,1:T(4,128)} %param.53) | copy-start | bytes 8116
  107.1 56.0 %copy-start.26 = (f32[2,128]{1,0:T(2,128)S(1)}, f32[2,128]{1,0:T(2,128)}, u32[]{:S(2)}) copy-start(f32[2,128]{1,0:T(2,128)} %param.45) | copy-start | bytes 3076
  107.1 56.0 %copy-start.29 = (f32[2,128]{1,0:T(2,128)S(1)}, f32[2,128]{1,0:T(2,128)}, u32[]{:S(2)}) copy-start(f32[2,128]{1,0:T(2,128)} %param.46) | copy-start | bytes 3076
  107.1 56.0 %copy-start.30 = (f32[2,128]{1,0:T(2,128)S(1)}, f32[2,128]{1,0:T(2,128)}, u32[]{:S(2)}) copy-start(f32[2,128]{1,0:T(2,128)} %param.47) | copy-start | bytes 3076
  107.1 56.7 %copy-start.23 = (f32[512]{0:T(512)S(1)}, f32[512]{0:T(512)}, u32[]{:S(2)}) copy-start(f32[512]{0:T(512)} %param.48) | copy-start | bytes 6148
  107.2 56.7 %copy-start.27 = (f32[512]{0:T(512)S(1)}, f32[512]{0:T(512)}, u32[]{:S(2)}) copy-start(f32[512]{0:T(512)} %param.49) | copy-start | bytes 6148
  107.2 56.7 %copy-start.28 = (f32[512]{0:T(512)S(1)}, f32[512]{0:T(512)}, u32[]{:S(2)}) copy-start(f32[512]{0:T(512)} %param.50) | copy-start | bytes 6148
  107.2 57.3 %copy-start.8 = (f32[16,3,128]{2,0,1:T(8,128)S(1)}, f32[16,3,128]{2,0,1:T(8,128)}, u32[]{:S(2)}) copy-start(f32[16,3,128]{2,0,1:T(8,128)} %param.30) | copy-start | bytes 73732
  107.2 57.3 %copy-start.17 = (f32[16,3,128]{2,0,1:T(8,128)S(1)}, f32[16,3,128]{2,0,1:T(8,128)}, u32[]{:S(2)}) copy-start(f32[16,3,128]{2,0,1:T(8,128)} %param.31) | copy-start | bytes 73732
  107.2 57.3 %copy-start.18 = (f32[16,3,128]{2,0,1:T(8,128)S(1)}, f32[16,3,128]{2,0,1:T(8,128)}, u32[]{:S(2)}) copy-start(f32[16,3,128]{2,0,1:T(8,128)} %param.32) | copy-start | bytes 73732
  107.2 57.9 %copy-start.6 = (f32[512,16]{0,1:T(8,128)S(1)}, f32[512,16]{0,1:T(8,128)}, u32[]{:S(2)}) copy-start(f32[512,16]{0,1:T(8,128)} %param.39) | copy-start | bytes 98308
  107.2 57.9 %copy-start.10 = (f32[512,16]{0,1:T(8,128)S(1)}, f32[512,16]{0,1:T(8,128)}, u32[]{:S(2)}) copy-start(f32[512,16]{0,1:T(8,128)} %param.40) | copy-start | bytes 98308
  107.2 57.9 %copy-start.11 = (f32[512,16]{0,1:T(8,128)S(1)}, f32[512,16]{0,1:T(8,128)}, u32[]{:S(2)}) copy-start(f32[512,16]{0,1:T(8,128)} %param.41) | copy-start | bytes 98308
  107.3 58.6 %copy-start.7 = (f32[16,512]{1,0:T(8,128)S(1)}, f32[16,512]{1,0:T(8,128)}, u32[]{:S(2)}) copy-start(f32[16,512]{1,0:T(8,128)} %param.36) | copy-start | bytes 98308
  107.3 58.5 %copy-start.12 = (f32[16,512]{1,0:T(8,128)S(1)}, f32[16,512]{1,0:T(8,128)}, u32[]{:S(2)}) copy-start(f32[16,512]{1,0:T(8,128)} %param.37) | copy-start | bytes 98308
  107.3 58.5 %copy-start.13 = (f32[16,512]{1,0:T(8,128)S(1)}, f32[16,512]{1,0:T(8,128)}, u32[]{:S(2)}) copy-start(f32[16,512]{1,0:T(8,128)} %param.38) | copy-start | bytes 98308
  107.3 59.2 %copy-start.9 = (f32[6,512]{1,0:T(8,128)S(1)}, f32[6,512]{1,0:T(8,128)}, u32[]{:S(2)}) copy-start(f32[6,512]{1,0:T(8,128)} %vec.1) | copy-start | bytes 36868
  107.3 59.2 %copy-start.19 = (f32[6,512]{1,0:T(8,128)S(1)}, f32[6,512]{1,0:T(8,128)}, u32[]{:S(2)}) copy-start(f32[6,512]{1,0:T(8,128)} %param.43) | copy-start | bytes 36868
  107.3 59.2 %copy-start.20 = (f32[6,512]{1,0:T(8,128)S(1)}, f32[6,512]{1,0:T(8,128)}, u32[]{:S(2)}) copy-start(f32[6,512]{1,0:T(8,128)} %param.44) | copy-start | bytes 36868
  107.3 59.8 %copy-start.14 = (f32[128,16]{0,1:T(8,128)S(1)}, f32[128,16]{0,1:T(8,128)}, u32[]{:S(2)}) copy-start(f32[128,16]{0,1:T(8,128)} %param.33) | copy-start | bytes 24580
  107.3 59.8 %copy-start.21 = (f32[128,16]{0,1:T(8,128)S(1)}, f32[128,16]{0,1:T(8,128)}, u32[]{:S(2)}) copy-start(f32[128,16]{0,1:T(8,128)} %param.34) | copy-start | bytes 24580
  107.4 59.8 %copy-start.22 = (f32[128,16]{0,1:T(8,128)S(1)}, f32[128,16]{0,1:T(8,128)}, u32[]{:S(2)}) copy-start(f32[128,16]{0,1:T(8,128)} %param.35) | copy-start | bytes 24580
  161.3 1.2 copy-start.1

commit v2 on v0

v2 whole, which is shorter than its diff:
```python
import types

import jax
import jax.numpy as jnp
from jax import lax
from jax.experimental import pallas as pl
from jax.experimental.pallas import tpu as pltpu
from jax.sharding import PartitionSpec as P

MESH = pl.DeviceIdType.MESH
LOW = jnp.bfloat16
FULL = jnp.float32
EPS = 1e-5
SCALE = 32.0 ** -0.5
BLOCKED = -1e30
STEP = 10
REL = 169
BETA_ONE = 0.9
BETA_TWO = 0.999
ADAM_EPS = 1e-08
RATE_MATRIX = 0.1
RATE_VECTOR = 0.2
RATE_TABLE = 0.5
WEIGHT_DECAY = 0.05
ORDERS = ((0, 1, 2), (1, 2, 0), (2, 0, 1))
SUMS = (((0, 1, 2), (1, 0, 2), (1, 0, 2)), ((0, 1, 2), (1, 0, 2), (0, 1, 2)))
WIDTHS = (128, 384)


class Place:
    def __init__(self):
        f = lax.axis_index("fsdp")
        self.t = lax.axis_index("tensor")
        x, y = f % 4, f // 8
        z = ((f // 4) % 2) * 2 + self.t // 2
        self.core = self.t % 2
        self.at = (x, y, z)
        mate = (x, y, (z // 2) * 2 + 1 - z % 2)
        self.sibling = self.device(core=1 - self.core)
        self.z_mate = self.device(mate)
        self.across = self.device(mate, 1 - self.core)
        self.mate_t = (1 - z % 2) * 2 + self.core

    def device(self, at=None, core=None):
        x, y, z = self.at if at is None else at
        core = self.core if core is None else core
        return (y * 8 + (z // 2) * 4 + x, (z % 2) * 2 + core)

    def along(self, axis, by):
        at = list(self.at)
        at[axis] = (at[axis] + by + 4) % 4
        return self.device(at)


def block_of(ref, lead, place, core, full, axis=None, shift=0):
    whole = slice(None)
    at = list(place.at)
    if axis is not None:
        at[axis] = (at[axis] + shift + 4) % 4
    x, y, z = at
    x = whole if 0 in full else x
    y = whole if 1 in full else y
    low, high = (whole, whole) if 2 in full else (z % 2, z // 2)
    return ref.at[(*lead, low, core, y, high, x)] if core is not None else ref.at[(*lead, low, y, high, x)]


def block_dims(full):
    return tuple(size for axis, size in ((2, 2), (1, 4), (2, 2), (0, 4)) if axis in full)


def each(dims, fn):
    outer = dims[:-1]
    count = 1
    for size in outer:
        count *= size
    if count == 1:
        fn((0,) * len(outer))
        return

    def body(n, _):
        index = []
        for size in reversed(outer):
            index.append(n % size)
            n = n // size
        fn(tuple(reversed(index)))
        return 0

    lax.fori_loop(0, count, body, 0)


def mm(a, b):
    return lax.dot_general(a, b, (((1,), (0,)), ((), ())), preferred_element_type=FULL)


def mm_nt(a, b):
    return lax.dot_general(a, b, (((1,), (1,)), ((), ())), preferred_element_type=FULL)


def mm_tn(a, b):
    return lax.dot_general(a, b, (((0,), (0,)), ((), ())), preferred_element_type=FULL)


def three_lows(a):
    high = a.astype(LOW)
    rest = a - high.astype(FULL)
    middle = rest.astype(LOW)
    last = (rest - middle.astype(FULL)).astype(LOW)
    return jnp.concatenate([high, middle, last], axis=0)


def normed(v):
    center = v - jnp.mean(v, axis=-1, keepdims=True)
    r = lax.rsqrt(jnp.mean(center * center, axis=-1, keepdims=True) + EPS)
    return center * r, r


def norm_back(n, x, r, offset):
    q = n * (1.0 + offset)
    return r * (q - jnp.mean(q, axis=-1, keepdims=True) - x * jnp.mean(q * x, axis=-1, keepdims=True))


def gelu_parts(u):
    size = jnp.abs(u)
    k = 1.0 / (1.0 + (0.3275911 * 0.7071067811865476) * size)
    bell = jnp.exp(-0.5 * u * u)
    poly = k * (0.254829592 + k * (-0.284496736 + k * (1.421413741 + k * (-1.453152027 + k * 1.061405429))))
    tail = 0.5 * poly * bell
    share = jnp.where(u < 0, tail, 1.0 - tail)
    return u * share, share + u * bell * 0.3989422804014327


def lane_mask(h):
    lane = lax.broadcasted_iota(jnp.int32, (128, 128), 1)
    return (lane >= h * 32) & (lane < h * 32 + 32)


def keep(mask, a):
    return jnp.where(mask, a, jnp.zeros_like(a))


def spans():
    for image in range(2):
        for r in range(14):
            for side in range(2):
                window = image * 4 + (r // 7) * 2 + side
                yield image, r * 14 + side * 7, window * 64 + (r % 7) * 7


def block_kernel(ref):
    images, cotangents, vec, idx = ref.images, ref.cotangents, ref.vec, ref.idx
    w = (ref.w1, ref.w2)
    g = (ref.g1, ref.g2)
    sib = (ref.sib1, ref.sib2)
    gs, small, steps = ref.gs, ref.small, ref.steps
    tok, cot, cot_low, cot_t = ref.tok, ref.cot, ref.cot_low, ref.cot_t
    n1, n1_t, x1, r1 = ref.n1, ref.n1_t, ref.x1, ref.r1
    n2, n2_t, x2, r2 = ref.n2, ref.n2_t, ref.x2, ref.r2
    qkv, probs, att, mid, hid, gpre = ref.qkv, ref.probs, ref.att, ref.mid, ref.hid, ref.gpre
    gmid, gml, gml_t, dqkv = ref.gmid, ref.gml, ref.gml_t, ref.dqkv
    onehot, spread, bias, dsum, table = ref.onehot, ref.spread, ref.bias, ref.dsum, ref.table
    stage, field, outs = ref.stage, ref.field, ref.outs
    local = ref.local_sem

    place = Place()
    t_own, core = place.t, place.core
    barrier = pltpu.get_barrier_semaphore()
    partners = [place.along(axis, by) for axis in range(3) for by in (1, 2, 3)] + [place.sibling, place.across]
    for device in partners:
        pl.semaphore_signal(barrier, inc=1, device_id=device, device_id_type=MESH)

    copies_in = [
        pltpu.make_async_copy(images, ref.img, local.at[0]),
        pltpu.make_async_copy(cotangents, ref.cimg, local.at[1]),
    ]
    for copy in copies_in:
        copy.start()

    sends = []

    def send(src, dst, out, into, device):
        copy = pltpu.make_async_remote_copy(src, dst, out, into, device, MESH)
        copy.start()
        sends.append(copy)

    def wait_in(block, out, into):
        pltpu.make_async_remote_copy(block, block, out, into, place.sibling, MESH).wait_recv()

    x, y, z = place.at
    own = (z % 2, core, y, z // 2, x)
    for p in range(3):
        w[0][(p, *own)] = ref.attn[p].astype(LOW)
    proj, up, down = ref.proj[...].astype(LOW), ref.up[...].astype(LOW), ref.down[...].astype(LOW)
    w[1][(0, *own)] = jnp.concatenate([proj, up[:, 0:256]], axis=1)
    w[1][(1, *own)] = jnp.concatenate([up[:, 256:512], down[:, 0:128]], axis=1)
    w[1][(2, *own)] = down[:, 128:512]
    mine = gs.at[t_own]
    mine[...] = jnp.zeros((16, 128), FULL)
    mine[0:4, :] = ref.rel[:, 0:128]
    mine[4:8, 0 : REL - 128] = ref.rel[:, 128:REL]
    mine[8:10, :] = ref.head[...]
    for k in range(4):
        mine[10 + k : 11 + k, :] = ref.unit[:, k * 128 : (k + 1) * 128]

    pl.semaphore_wait(barrier, len(partners))

    in_sem, out_sem, sib_in, sib_out = ref.w_in, ref.w_out, ref.ws_in, ref.ws_out

    def gather_start(b, phase):
        for p in range(3):
            axis, done = ORDERS[p][phase], ORDERS[p][:phase]
            block = block_of(w[b], (p,), place, core, done)
            for shift in (1, 3, 2):
                at = (b, p, phase, shift - 1)
                send(block, block, out_sem.at[at], in_sem.at[at], place.along(axis, shift))
            if phase == 2:
                send(block, block, sib_out.at[b, p, 0], sib_in.at[b, p, 0], place.sibling)

    def gather_finish(b, phase, shifts=(1, 3, 2)):
        for shift in shifts:
            for p in range(3):
                axis, done = ORDERS[p][phase], ORDERS[p][:phase]
                block = block_of(w[b], (p,), place, core, done, axis, -shift)
                at = (b, p, phase, shift - 1)
                wait_in(block, out_sem.at[at], in_sem.at[at])
                if phase == 2:
                    send(block, block, sib_out.at[b, p, shift], sib_in.at[b, p, shift], place.sibling)

    def gather_last(b):
        for p in range(3):
            axis, done = ORDERS[p][2], ORDERS[p][:2]
            for shift in range(4):
                block = block_of(w[b], (p,), place, 1 - core, done, axis, -shift)
                wait_in(block, sib_out.at[b, p, shift], sib_in.at[b, p, shift])

    mates = (place.sibling, place.z_mate, place.across)
    mate_ts = (t_own + 1 - 2 * core, place.mate_t, (1 - z % 2) * 2 + 1 - core)
    gather_start(0, 0)
    gather_start(1, 0)
    for k in range(3):
        send(mine, mine, ref.s_out.at[k], ref.s_in.at[k], mates[k])

    wide = ref.wide
    wide[...] = jnp.full((56, 128), -1, jnp.int32)
    wide[0:49, 0:49] = idx[...]
    wide[0:49, 64:113] = idx[...]
    row_id = lax.broadcasted_iota(jnp.int32, (256, 128), 0)
    for i in range(49):
        onehot[:, i * 128 : (i + 1) * 128] = (row_id == wide[i : i + 1, :]).astype(FULL).astype(LOW)
    small[...] = jnp.zeros((16, 768), FULL)
    tok[...] = jnp.zeros((512, 512), FULL)
    cot[...] = jnp.zeros((512, 512), FULL)
    gather_finish(0, 0)
    gather_start(0, 1)
    gather_finish(1, 0)
    gather_start(1, 1)
    for n, (source, copy, dst) in enumerate(zip((ref.img, ref.cimg), copies_in, (tok, cot))):
        copy.wait()
        if n == 1:
            gather_finish(0, 1)
            gather_start(0, 2)

        def widen(k, _):
            rows = pl.ds(pl.multiple_of(k * 112, 112), 112)
            for k4 in range(4):
                stage[k4, rows, :] = source[rows, k4 * 128 : (k4 + 1) * 128].astype(FULL)
            return 0

        lax.fori_loop(0, 14, widen, 0)
        for image, first, top in spans():
            for k in range(4):
                dst[top : top + 7, k * 128 : (k + 1) * 128] = stage[
                    k, pl.ds(first * 8 + image + 2 * t_own, 7, stride=8), :
                ]
    gather_finish(1, 1)

    def start(k, _):
        rows = pl.ds(pl.multiple_of(k * 64, 64), 64)
        xs, r = normed(tok[rows, :])
        x1[rows, :] = xs
        r1[rows, :] = r
        n1[rows, :] = (xs * (1.0 + vec[0:1, :]) + vec[1:2, :]).astype(LOW)
        c = cot[rows, :]
        cot_low[rows, :] = c.astype(LOW)
        small[5:6, 0:512] += jnp.sum(c, axis=0, keepdims=True)
        return 0

    lax.fori_loop(0, 8, start, 0)
    for k in range(3):
        wait_in(gs.at[mate_ts[k]], ref.s_out.at[k], ref.s_in.at[k])
    for t in range(4):
        table[t * 4 : t * 4 + 4, 0:128] = gs[t, 0:4, :]
        table[t * 4 : t * 4 + 4, 128:256] = gs[t, 4:8, :]
    spread[...] = mm(three_lows(table[...]), onehot[...])
    lane = lax.broadcasted_iota(jnp.int32, (16, 128), 1)
    low_side = lane < 49
    high_side = (lane >= 64) & (lane < 113)
    for i in range(64):
        if i < 49:
            at = slice(i * 128, (i + 1) * 128)
            line = spread[0:16, at] + spread[16:32, at] + spread[32:48, at]
        else:
            line = jnp.zeros((16, 128), FULL)
        bias[i * 16 : (i + 1) * 16, :] = jnp.where(low_side, line, BLOCKED)
        bias[(64 + i) * 16 : (65 + i) * 16, :] = jnp.where(high_side, line, BLOCKED)
    gather_finish(0, 2, (1, 3))
    gather_start(1, 2)
    n1_t[...] = n1[...].T
    cot_t[...] = cot_low[...].T
    gather_finish(0, 2, (2,))
    gather_last(0)

    def columns(b, p, t, a, z):
        return w[b][p, t // 2, t % 2, :, :, :, :, a:z].reshape(512, z - a)

    def w_qkv(t):
        return jnp.concatenate([columns(0, c, t, 0, 128) for c in range(3)], axis=1)

    def w_proj(t):
        return columns(1, 0, t, 0, 128)

    def w_up(t):
        return jnp.concatenate([columns(1, 0, t, 128, 384), columns(1, 1, t, 0, 256)], axis=1)

    def w_down(t):
        return jnp.concatenate([columns(1, 1, t, 256, 384), columns(1, 2, t, 0, 384)], axis=1)

    def put_grad(b, p, t, a, value):
        g[b][p, t // 2, t % 2, :, :, :, :, a : a + value.shape[1]] = value.astype(LOW).reshape(
            4, 2, 4, 16, value.shape[1]
        )

    def forward(t, _):
        mixed = mm(n1[...], w_qkv(t))
        q_bias, v_bias = gs[t, 8:9, :], gs[t, 9:10, :]
        qkv[t, 0] = (mixed[:, 0:128] + q_bias).astype(LOW)
        qkv[t, 1] = mixed[:, 128:256].astype(LOW)
        qkv[t, 2] = (mixed[:, 256:384] + v_bias).astype(LOW)
        for wp in range(4):
            rows = slice(wp * 128, (wp + 1) * 128)
            q, k, v = qkv[t, 0, rows], qkv[t, 1, rows], qkv[t, 2, rows]
            ps, vs = [], []
            for h in range(4):
                mask = lane_mask(h)
                s = mm_nt(keep(mask, q), k) * SCALE + bias[pl.ds(t * 4 + h, 128, stride=16), :]
                e = jnp.exp(s - jnp.max(s, axis=-1, keepdims=True))
                p = (e / jnp.sum(e, axis=-1, keepdims=True)).astype(LOW)
                probs[t, wp, h] = p
                ps.append(p)
                vs.append(keep(mask, v))
            att[t, rows] = mm(jnp.concatenate(ps, axis=1), jnp.concatenate(vs, axis=0)).astype(LOW)
        return 0

    lax.fori_loop(0, 3, forward, 0)
    gather_finish(1, 2, (1, 3))
    lax.fori_loop(3, 4, forward, 0)
    gather_finish(1, 2, (2,))
    gather_last(1)

    def second(k, _):
        rows = pl.ds(pl.multiple_of(k * 128, 128), 128)
        acc = tok[rows, :] + vec[2:3, :]
        for t in range(4):
            acc = acc + mm_nt(att[t, rows, :], w_proj(t))
        mid[rows, :] = acc
        xs, r = normed(acc)
        x2[rows, :] = xs
        r2[rows, :] = r
        n2[rows, :] = (xs * (1.0 + vec[3:4, :]) + vec[4:5, :]).astype(LOW)
        return 0

    lax.fori_loop(0, 4, second, 0)
    n2_t[...] = n2[...].T

    def feed(t, _):
        unit = jnp.concatenate([gs[t, 10 + k : 11 + k, :] for k in range(4)], axis=1)
        up_t, down_t = w_up(t), w_down(t)

        def rows_of(k, total):
            rows = pl.ds(pl.multiple_of(k * 128, 128), 128)
            pre = mm(n2[rows, :], up_t) + unit
            value, slope = gelu_parts(pre)
            hid[t, rows, :] = value.astype(LOW)
            grad = mm(cot_low[rows, :], down_t) * slope
            gpre[t, rows, :] = grad.astype(LOW)
            return total + jnp.sum(grad, axis=0, keepdims=True)

        small[pl.ds(8 + t, 1), 0:512] = lax.fori_loop(0, 4, rows_of, jnp.zeros((1, 512), FULL))
        grad_up = mm(n2_t[...], gpre[t])
        put_grad(1, 0, t, 128, grad_up[:, 0:256])
        put_grad(1, 1, t, 0, grad_up[:, 256:512])
        grad_down = mm(cot_t[...], hid[t])
        put_grad(1, 1, t, 256, grad_down[:, 0:128])
        put_grad(1, 2, t, 0, grad_down[:, 128:512])
        return 0

    lax.fori_loop(0, 4, feed, 0)

    g_in, g_out, gs_in, gs_out = ref.g_in, ref.g_out, ref.gs_in, ref.gs_out
    slot = ref.slots

    def sum_core(b, p):
        axis, full = SUMS[b][p][0], SUMS[b][p][1:]
        for shift in (1, 3, 2, 0):
            src = block_of(g[b], (p,), place, 1 - core, full, axis, shift)
            dst = block_of(sib[b], (p,), place, None, full, axis, shift)
            send(src, dst, gs_out.at[b, p, shift], gs_in.at[b, p, shift], place.sibling)

    def sum_start(b, p, phase):
        axis, full = SUMS[b][p][phase], SUMS[b][p][phase + 1 :]
        for shift in (1, 3, 2, 0):
            here = block_of(g[b], (p,), place, core, full, axis, shift)
            if phase == 0:
                there = block_of(sib[b], (p,), place, None, full, axis, shift)
                wait_in(there, gs_out.at[b, p, shift], gs_in.at[b, p, shift])

                def add(index):
                    here[index] = here[index] + there[index]

                each(block_dims(full), add)
            if shift:
                at = (b, p, phase, shift - 1)
                send(here, slot[b, p, phase].at[shift - 1], g_out.at[at], g_in.at[at], place.along(axis, shift))

    def sum_finish(b, p, phase):
        axis, full = SUMS[b][p][phase], SUMS[b][p][phase + 1 :]
        here = block_of(g[b], (p,), place, core, full)
        came = [slot[b, p, phase].at[k] for k in range(3)]
        for k in range(3):
            wait_in(came[k], g_out.at[b, p, phase, k], g_in.at[b, p, phase, k])

        def total(index):
            one, two, three = (c[index].astype(FULL) for c in came)
            return (here[index].astype(FULL) + one) + (two + three)

        if phase == 2:
            return total(())

        def add(index):
            here[index] = total(index).astype(LOW)

        each(block_dims(full), add)
        return None

    sum_core(1, 1)
    sum_core(1, 2)

    def third(k, _):
        rows = pl.ds(pl.multiple_of(k * 128, 128), 128)
        out = mid[rows, :] + vec[5:6, :]
        n = jnp.zeros((128, 512), FULL)
        for t in range(4):
            out = out + mm_nt(hid[t, rows, :], w_down(t))
            n = n + mm_nt(gpre[t, rows, :], w_up(t))
        mid[rows, :] = out
        xs = x2[rows, :]
        grad = cot[rows, :] + norm_back(n, xs, r2[rows, :], vec[3:4, :])
        gmid[rows, :] = grad
        gml[rows, :] = grad.astype(LOW)
        small[2:3, 0:512] += jnp.sum(grad, axis=0, keepdims=True)
        small[3:4, 0:512] += jnp.sum(n * xs, axis=0, keepdims=True)
        small[4:5, 0:512] += jnp.sum(n, axis=0, keepdims=True)
        return 0

    lax.fori_loop(0, 4, third, 0)
    gml_t[...] = gml[...].T

    def proj_grad(t, _):
        put_grad(1, 0, t, 0, mm(gml_t[...], att[t]))
        return 0

    lax.fori_loop(0, 4, proj_grad, 0)
    sum_core(1, 0)

    o_in, o_out = ref.o_in, ref.o_out

    def give(n, half, src):
        rows = pl.ds(half * 208, 208)
        for image, first, top in spans():
            if image == half:
                field[half * 208 + first : half * 208 + first + 7, :] = src[top : top + 7, :]
        outs[n, t_own, rows, :] = field[rows, :].astype(LOW)
        block = outs.at[n, t_own, rows]
        send(block, block, o_out.at[n, half, 1], o_in.at[n, half, 1], place.z_mate)
        send(block, block, o_out.at[n, half, 0], o_in.at[n, half, 0], place.sibling)

    def came(n, half, kind):
        t = mate_ts[kind]
        block = outs.at[n, t, pl.ds(half * 208, 208)]
        wait_in(block, o_out.at[n, half, kind], o_in.at[n, half, kind])
        if kind == 1:
            send(block, block, o_out.at[n, half, 2], o_in.at[n, half, 2], place.sibling)

    def take(n, half, t):
        field[0:208, :] = outs[n, t, half * 208 : half * 208 + 208, :].astype(FULL)
        for k in range(4):
            stage[k, pl.ds(2 * t + half, 196, stride=8), :] = field[0:196, k * 128 : (k + 1) * 128]

    def take_near(n):
        for half in range(2):
            take(n, half, t_own)
            came(n, half, 0)
            take(n, half, mate_ts[0])

    def take_far(n):
        for half in range(2):
            take(n, half, mate_ts[1])
        for half in range(2):
            came(n, half, 2)
            take(n, half, mate_ts[2])

    field[...] = jnp.zeros((416, 512), FULL)
    for p in (1, 2, 0):
        sum_start(1, p, 0)
    give(0, 0, mid)
    give(0, 1, mid)

    def backward(t, _):
        ga = mm(gml[...], w_proj(t)).astype(LOW)
        sums = [jnp.zeros((128, 128), FULL) for _ in range(4)]
        sum_q = jnp.zeros((1, 128), FULL)
        sum_v = jnp.zeros((1, 128), FULL)
        for wp in range(4):
            rows = slice(wp * 128, (wp + 1) * 128)
            q, k, v, grad = qkv[t, 0, rows], qkv[t, 1, rows], qkv[t, 2, rows], ga[rows]
            dss, ps, ks, qs, gg = [], [], [], [], []
            for h in range(4):
                mask = lane_mask(h)
                p_low = probs[t, wp, h]
                p = p_low.astype(FULL)
                gh = keep(mask, grad)
                dp = mm_nt(gh, v)
                ds = (p * (dp - jnp.sum(dp * p, axis=-1, keepdims=True))).astype(LOW)
                sums[h] = sums[h] + ds.astype(FULL)
                dss.append(ds)
                ps.append(p_low)
                ks.append(keep(mask, k))
                qs.append(keep(mask, q))
                gg.append(gh)
            dq = (mm(jnp.concatenate(dss, axis=1), jnp.concatenate(ks, axis=0)) * SCALE).astype(LOW)
            dk = (mm_tn(jnp.concatenate(dss, axis=0), jnp.concatenate(qs, axis=0)) * SCALE).astype(LOW)
            dv = mm_tn(jnp.concatenate(ps, axis=0), jnp.concatenate(gg, axis=0)).astype(LOW)
            dqkv[t, rows, 0:128] = dq
            dqkv[t, rows, 128:256] = dk
            dqkv[t, rows, 256:384] = dv
            sum_q = sum_q + jnp.sum(dq.astype(FULL), axis=0, keepdims=True)
            sum_v = sum_v + jnp.sum(dv.astype(FULL), axis=0, keepdims=True)
        for h in range(4):
            dsum[pl.ds(t * 4 + h, 128, stride=16), :] = sums[h]
        at = pl.ds(pl.multiple_of(t * 128, 128), 128)
        small[6:7, at] = sum_q
        small[7:8, at] = sum_v
        grad = mm(n1_t[...], dqkv[t])
        for c in range(3):
            put_grad(0, c, t, 0, grad[:, c * 128 : (c + 1) * 128])
        return 0

    lax.fori_loop(0, 4, backward, 0)
    for p in range(3):
        sum_core(0, p)
    lines = []
    for i in range(49):
        lines.append(three_lows(dsum[i * 16 : (i + 1) * 16, :] + dsum[(64 + i) * 16 : (65 + i) * 16, :]))
    table_sum = mm_nt(jnp.concatenate(lines, axis=1), onehot[...])
    small[:, 512:768] = table_sum[0:16] + table_sum[16:32] + table_sum[32:48]

    def last(k, _):
        rows = pl.ds(pl.multiple_of(k * 128, 128), 128)
        n = jnp.zeros((128, 512), FULL)
        for t in range(4):
            n = n + mm_nt(dqkv[t, rows, :], w_qkv(t))
        xs = x1[rows, :]
        gmid[rows, :] += norm_back(n, xs, r1[rows, :], vec[0:1, :])
        small[0:1, 0:512] += jnp.sum(n * xs, axis=0, keepdims=True)
        small[1:2, 0:512] += jnp.sum(n, axis=0, keepdims=True)
        return 0

    lax.fori_loop(0, 2, last, 0)
    give(1, 0, gmid)
    for p in range(3):
        sum_start(0, p, 0)
    lax.fori_loop(2, 4, last, 0)
    give(1, 1, gmid)

    n_in, n_out = ref.n_in, ref.n_out

    def small_start(k):
        if k < 3:
            block = steps.at[k, place.at[k]]
            for shift in (1, 3, 2):
                send(block, block, n_out.at[k, shift - 1], n_in.at[k, shift - 1], place.along(k, shift))
        else:
            block = steps.at[3, core]
            send(block, block, n_out.at[3, 0], n_in.at[3, 0], place.sibling)

    def small_finish(k):
        if k < 3:
            for shift in (1, 3, 2):
                at = (place.at[k] - shift + 4) % 4
                wait_in(steps.at[k, at], n_out.at[k, shift - 1], n_in.at[k, shift - 1])
            return (steps[k, 0] + steps[k, 1]) + (steps[k, 2] + steps[k, 3])
        wait_in(steps.at[3, 1 - core], n_out.at[3, 0], n_in.at[3, 0])
        return steps[3, 0] + steps[3, 1]

    def small_next(k):
        value = small_finish(k)
        steps[k + 1, place.at[k + 1] if k < 2 else core] = value
        small_start(k + 1)

    steps[0, place.at[0]] = small[...]
    small_start(0)
    for half in range(2):
        came(0, half, 1)
    take_near(0)
    for p in range(3):
        sum_finish(1, p, 0)
        sum_start(1, p, 1)
    for p in range(3):
        sum_finish(0, p, 0)
        sum_start(0, p, 1)
    small_next(0)
    take_far(0)

    def narrow(k, _):
        rows = pl.ds(pl.multiple_of(k * 112, 112), 112)
        for k4 in range(4):
            ref.block_out[rows, k4 * 128 : (k4 + 1) * 128] = stage[k4, rows, :].astype(LOW)
        return 0

    lax.fori_loop(0, 14, narrow, 0)
    for p in range(3):
        sum_finish(0, p, 1)
        sum_start(0, p, 2)
    small_next(1)
    for p in range(3):
        sum_finish(1, p, 1)
        sum_start(1, p, 2)
    take_near(1)
    for half in range(2):
        came(1, half, 1)
    for p in range(3):
        ref.attn_grad[p] = sum_finish(0, p, 2)
    small_next(2)
    first, second_, third_ = (sum_finish(1, p, 2) for p in range(3))
    ref.proj_grad[...] = first[:, 0:128]
    ref.up_grad[:, 0:256] = first[:, 128:384]
    ref.up_grad[:, 256:512] = second_[:, 0:256]
    ref.down_grad[:, 0:128] = second_[:, 256:384]
    ref.down_grad[:, 128:512] = third_
    take_far(1)
    ref.total[...] = small_finish(3)
    results = []
    for k in range(4):
        lanes = ref.images_grad.at[:, pl.ds(k * 128, 128)]
        results.append(pltpu.make_async_copy(stage.at[k], lanes, local.at[k]))
        results[k].start()
    for copy in sends:
        copy.wait_send()
    for copy in results:
        copy.wait()


def run_block(images, cotangents, vec, idx, attn, proj, up, down, rel, head, unit):
    whole = pl.BlockSpec(memory_space=pltpu.VMEM)
    anywhere = pl.BlockSpec(memory_space=pl.ANY)
    ins = dict(
        images=anywhere, cotangents=anywhere, vec=whole, idx=whole, attn=whole, proj=whole,
        up=whole, down=whole, rel=whole, head=whole, unit=whole,
    )
    results = dict(
        block_out=((1568, 512), LOW, whole),
        images_grad=((1568, 512), FULL, anywhere),
        attn_grad=((3, 16, 128), FULL, whole),
        proj_grad=((16, 128), FULL, whole),
        up_grad=((16, 512), FULL, whole),
        down_grad=((16, 512), FULL, whole),
        total=((16, 768), FULL, whole),
    )
    square = (512, 512)
    scratch = dict(
        img=pltpu.VMEM((1568, 512), LOW),
        cimg=pltpu.VMEM((1568, 512), LOW),
        w1=pltpu.VMEM((3, 2, 2, 4, 2, 4, 16, 128), LOW),
        w2=pltpu.VMEM((3, 2, 2, 4, 2, 4, 16, 384), LOW),
        g1=pltpu.VMEM((3, 2, 2, 4, 2, 4, 16, 128), LOW),
        g2=pltpu.VMEM((3, 2, 2, 4, 2, 4, 16, 384), LOW),
        sib1=pltpu.VMEM((3, 2, 4, 2, 4, 16, 128), LOW),
        sib2=pltpu.VMEM((3, 2, 4, 2, 4, 16, 384), LOW),
        gs=pltpu.VMEM((4, 16, 128), FULL),
        small=pltpu.VMEM((16, 768), FULL),
        steps=pltpu.VMEM((4, 4, 16, 768), FULL),
        qkv=pltpu.VMEM((4, 3, 512, 128), LOW),
        probs=pltpu.VMEM((4, 4, 4, 128, 128), LOW),
        att=pltpu.VMEM((4, 512, 128), LOW),
        hid=pltpu.VMEM((4, 512, 512), LOW),
        gpre=pltpu.VMEM((4, 512, 512), LOW),
        dqkv=pltpu.VMEM((4, 512, 384), LOW),
        onehot=pltpu.VMEM((256, 49 * 128), LOW),
        spread=pltpu.VMEM((48, 49 * 128), FULL),
        bias=pltpu.VMEM((2048, 128), FULL),
        dsum=pltpu.VMEM((2048, 128), FULL),
        table=pltpu.VMEM((16, 256), FULL),
        wide=pltpu.VMEM((56, 128), jnp.int32),
        stage=pltpu.VMEM((4, 1568, 128), FULL),
        field=pltpu.VMEM((416, 512), FULL),
        outs=pltpu.VMEM((2, 4, 416, 512), LOW),
        r1=pltpu.VMEM((512, 1), FULL),
        r2=pltpu.VMEM((512, 1), FULL),
    )
    full, low = pltpu.VMEM(square, FULL), pltpu.VMEM(square, LOW)
    scratch.update(tok=full, cot=full, x1=full, x2=full, mid=full, gmid=full)
    scratch.update(cot_low=low, cot_t=low, n1=low, n1_t=low, n2=low, n2_t=low, gml=low, gml_t=low)
    slots = {}
    for b in range(2):
        for p in range(3):
            for phase in range(3):
                slots[b, p, phase] = pltpu.VMEM((3, *block_dims(SUMS[b][p][phase + 1 :]), 16, WIDTHS[b]), LOW)
    sems = dict(
        local_sem=(4,), w_in=(2, 3, 3, 3), w_out=(2, 3, 3, 3), ws_in=(2, 3, 4), ws_out=(2, 3, 4),
        s_in=(3,), s_out=(3,), g_in=(2, 3, 3, 3), g_out=(2, 3, 3, 3), gs_in=(2, 3, 4), gs_out=(2, 3, 4),
        o_in=(2, 2, 3), o_out=(2, 2, 3), n_in=(4, 3), n_out=(4, 3),
    )
    for name, shape in sems.items():
        scratch[name] = pltpu.SemaphoreType.DMA(shape)
    names = [*ins, *results, *scratch]

    def kernel(*refs):
        named = dict(zip(names, refs))
        block_kernel(types.SimpleNamespace(**named, slots=dict(zip(slots, refs[len(names) :]))))

    return pl.pallas_call(
        kernel,
        out_shape=tuple(jax.ShapeDtypeStruct(shape, dtype) for shape, dtype, _ in results.values()),
        in_specs=list(ins.values()),
        out_specs=[spec for _, _, spec in results.values()],
        scratch_shapes=[*scratch.values(), *slots.values()],
        compiler_params=pltpu.CompilerParams(
            collective_id=0, has_side_effects=True, vmem_limit_bytes=63 * 2**20
        ),
        name="block_forward_backward",
    )(images, cotangents, vec, idx, attn, proj, up, down, rel, head, unit)


def adam_step(weight, grad, first, second, rate, decay):
    first_new = BETA_ONE * first + (1.0 - BETA_ONE) * grad
    second_new = BETA_TWO * second + (1.0 - BETA_TWO) * grad * grad
    first_hat = first_new / (1.0 - BETA_ONE**STEP)
    second_hat = second_new / (1.0 - BETA_TWO**STEP)
    updated = weight - rate * (first_hat / (jnp.sqrt(second_hat) + ADAM_EPS) + decay * weight)
    return (updated, first_new, second_new)


PARAMETERS = (
    ((3, 16, 128), RATE_MATRIX, WEIGHT_DECAY),
    ((16, 128), RATE_MATRIX, WEIGHT_DECAY),
    ((16, 512), RATE_MATRIX, WEIGHT_DECAY),
    ((16, 512), RATE_MATRIX, WEIGHT_DECAY),
    ((6, 512), RATE_VECTOR, 0.0),
    ((2, 128), RATE_VECTOR, 0.0),
    ((1, 512), RATE_VECTOR, 0.0),
    ((4, REL), RATE_TABLE, 0.0),
)


def update_kernel(*refs):
    refs = list(refs)

    def some(count):
        taken = refs[:count]
        del refs[:count]
        return taken

    results, grads, states = some(2), some(5), some(24)
    results_out, states_out = some(2), some(24)
    held, grads_in, states_in, states_new = some(2), some(5), some(24), some(24)
    sems_in, sems_out = refs
    arriving = []
    leaving = []
    for n, (source, page, target) in enumerate(zip(results, held, results_out)):
        for k in range(2):
            rows = pl.ds(k * 784, 784)
            at = 2 * n + k
            arriving.append(pltpu.make_async_copy(source.at[rows], page.at[rows], sems_in.at[29 + at]))
            leaving.append(pltpu.make_async_copy(page.at[rows], target.at[rows], sems_out.at[24 + at]))
    loads = [
        pltpu.make_async_copy(a, b, sems_in.at[n]) for n, (a, b) in enumerate(zip(grads + states, grads_in + states_in))
    ]
    for copy in loads + arriving:
        copy.start()
    for copy in loads:
        copy.wait()
    t = lax.axis_index("tensor")
    total = grads_in[4]

    def picked(pieces):
        value = pieces[3]
        for k in (2, 1, 0):
            value = jnp.where(t == k, pieces[k], value)
        return value

    small = (
        total[0:6, 0:512],
        picked([total[6:8, k * 128 : (k + 1) * 128] for k in range(4)]),
        picked([total[8 + k : 9 + k, 0:512] for k in range(4)]),
        picked([total[4 * k : 4 * k + 4, 512 : 512 + REL] for k in range(4)]),
    )
    for coming, going in zip(arriving, leaving):
        coming.wait()
        going.start()
    stores = []
    for n, (_, rate, decay) in enumerate(PARAMETERS):
        grad = grads_in[n][...] if n < 4 else small[n - 4]
        weight, first, second = (states_in[3 * n + k][...] for k in range(3))
        for k, value in enumerate(adam_step(weight, grad, first, second, rate, decay)):
            at = 3 * n + k
            states_new[at][...] = value
            copy = pltpu.make_async_copy(states_new[at], states_out[at], sems_out.at[at])
            copy.start()
            stores.append(copy)
    for copy in stores + leaving:
        copy.wait()


def update(results, grads, states):
    anywhere = pl.BlockSpec(memory_space=pl.ANY)
    shapes = [shape for shape, _, _ in PARAMETERS for _ in range(3)]
    inner = [pltpu.VMEM(shape, FULL) for shape in shapes]
    out_shape = [jax.ShapeDtypeStruct(a.shape, a.dtype) for a in results]
    out_shape += [jax.ShapeDtypeStruct(shape, FULL) for shape in shapes]
    return pl.pallas_call(
        update_kernel,
        out_shape=out_shape,
        in_specs=[anywhere] * 31,
        out_specs=[anywhere] * 26,
        scratch_shapes=[
            *[pltpu.VMEM(a.shape, a.dtype) for a in [*results, *grads]], *inner, *inner,
            pltpu.SemaphoreType.DMA((33,)), pltpu.SemaphoreType.DMA((28,)),
        ],
        compiler_params=pltpu.CompilerParams(vmem_limit_bytes=60 * 2**20),
        name="adam_update",
    )(*results, *grads, *states)


def on_device(
    images,
    out_grad,
    rel_index,
    attn_weight,
    attn_first,
    attn_second,
    proj_weight,
    proj_first,
    proj_second,
    up_weight,
    up_first,
    up_second,
    down_weight,
    down_first,
    down_second,
    vectors,
    vec_first,
    vec_second,
    head_bias,
    head_first,
    head_second,
    unit_bias,
    unit_first,
    unit_second,
    rel_table,
    table_first,
    table_second,
):
    def flat(field):
        return jnp.transpose(field, (1, 2, 0, 3)).reshape(1568, 512)

    def unflat(rows):
        return jnp.transpose(rows.reshape(14, 14, 8, 512), (2, 0, 1, 3))

    def turned(a):
        return jnp.transpose(a, (1, 0, 2))

    def row(a):
        return a.reshape(1, 512)

    def same(a):
        return a

    def flipped(a):
        return a.T

    ways = (turned, flipped, same, flipped, same, same, row, flipped)
    back = (turned, flipped, same, flipped, same, same, lambda a: a.reshape(512), flipped)
    groups = (
        (attn_weight, attn_first, attn_second),
        (proj_weight, proj_first, proj_second),
        (up_weight, up_first, up_second),
        (down_weight, down_first, down_second),
        (vectors, vec_first, vec_second),
        (head_bias, head_first, head_second),
        (unit_bias, unit_first, unit_second),
        (rel_table, table_first, table_second),
    )
    states = [way(a) for way, group in zip(ways, groups) for a in group]
    attn, proj, up, down, vec, head, unit, rel = states[::3]
    block, igrad, *grads = run_block(
        flat(images), flat(out_grad), vec, rel_index, attn, proj, up, down, rel, head, unit
    )
    block, igrad, *new = update((block, igrad), grads, states)
    news = [way(a) for way, at in zip(back, range(0, 24, 3)) for a in new[at : at + 3]]
    return (unflat(block), unflat(igrad), *news)


def solution(mesh):
    in_specs = (
        P("fsdp", None, None, None),
        P("fsdp", None, None, None),
        P(),
        P("fsdp", None, "tensor"),
        P("fsdp", None, "tensor"),
        P("fsdp", None, "tensor"),
        P("tensor", "fsdp"),
        P("tensor", "fsdp"),
        P("tensor", "fsdp"),
        P("fsdp", "tensor"),
        P("fsdp", "tensor"),
        P("fsdp", "tensor"),
        P("tensor", "fsdp"),
        P("tensor", "fsdp"),
        P("tensor", "fsdp"),
        P(),
        P(),
        P(),
        P(None, "tensor"),
        P(None, "tensor"),
        P(None, "tensor"),
        P("tensor"),
        P("tensor"),
        P("tensor"),
        P(None, "tensor"),
        P(None, "tensor"),
        P(None, "tensor"),
    )
    out_specs = (
        P("fsdp", None, None, None),
        P("fsdp", None, None, None),
        P("fsdp", None, "tensor"),
        P("fsdp", None, "tensor"),
        P("fsdp", None, "tensor"),
        P("tensor", "fsdp"),
        P("tensor", "fsdp"),
        P("tensor", "fsdp"),
        P("fsdp", "tensor"),
        P("fsdp", "tensor"),
        P("fsdp", "tensor"),
        P("tensor", "fsdp"),
        P("tensor", "fsdp"),
        P("tensor", "fsdp"),
        P(),
        P(),
        P(),
        P(None, "tensor"),
        P(None, "tensor"),
        P(None, "tensor"),
        P("tensor"),
        P("tensor"),
        P("tensor"),
        P(None, "tensor"),
        P(None, "tensor"),
        P(None, "tensor"),
    )
    return jax.shard_map(
        on_device, mesh=mesh, in_specs=in_specs, out_specs=out_specs, check_vma=False
    )
```

time: 769 us -> 103 us (0.13)
  waiting for transfers between devices: 482 us -> 0 us
  local copies, waits for them, and re-layouts: 113 us -> 0 us
  Pallas kernels: 0 us -> 102 us
  other arithmetic: 76.7 us -> 0 us
  matrix products: 66.6 us -> 0 us
  between operations: 15 us -> 0.84 us
  starting transfers between devices: 9.72 us -> 0 us
    psum x3 -> x0, waiting for transfers between devices: 254 us -> none  [the longest x1 109 us: on_device(): lax.psum(down_part, 'tensor')]
    reduce_scatter x1 -> x0, waiting for transfers between devices: 188 us -> none  [sum_together(): lax.psum_scatter(lines, axis, tiled=True).reshape(-1)]
    pallas_call x0 -> x2, Pallas kernels: none -> 102 us  [the longest x1 96.9 us: run_block(): pl.pallas_call(kernel, out_shape=tuple((jax.ShapeDtypeStruct(shape, dtype...]
    dot_general x20 -> x0, matrix products: 66.6 us -> none  [the longest x1 8.31 us: on_device(): jnp.einsum('wtf,wtd->fd', hidden_low, cot_low, preferred_element_type=ful...]
    reduce_sum x13 -> x0, other arithmetic: 40.4 us -> none  [the longest x4 18.1 us: layer_norm(): return center * lax.rsqrt(spread + NORM_EPS) * (1.0 + offset) + shift]
    all_gather x1 -> x0, waiting for transfers between devices: 40.1 us -> none  [rows_first(): result = lax.all_gather(both, axis, axis=0, tiled=True)]
    reshape x21 -> x0, local copies, waits for them, and re-layouts: 34.1 us -> none  [the longest x4 14.3 us: from_windows(): field.reshape(count, SIDE // WIN, SIDE // WIN, WIN, WIN, field.shape[-1])]
    dot_general x4 -> x0, local copies, waits for them, and re-layouts: 18.5 us -> none  [the longest x1 8.76 us: on_device(): jnp.einsum('wtf,wtd->fd', hidden_low, cot_low, preferred_element_type=ful...]
  transfers between devices with their start and end apart: 6 -> 0, of which waited for: 5 -> 0; matrix products, arithmetic and copies ran while one was open for 15% -> 0% of each run, Pallas kernels for 0% -> 0%
where the time goes in v2:
time: 103 us
  Pallas kernels  102 us (99%)
    pallas_call x1, Pallas kernels, run_block(): pl.pallas_call(kernel, out_shape=tuple((jax.ShapeDtypeStruct(shape, dtype...  96.9 us
    pallas_call x1, Pallas kernels, update(): pl.pallas_call(update_kernel, out_shape=out_shape, in_specs=[anywhere] *...  5.27 us

profile of v2, /device:TPU:1, one launch (start us, length us, event | category | flops | bytes accessed | tf_op | source)
XLA Modules:
  0.0 103.0 jit_solution(17338338822738405507)
XLA Ops:
  0.7 96.9 %block_forward_backward.1 = (bf16[1568,512]{1,0:T(8,128)(2,1)}, f32[1568,512]{1,0:T(8,128)}, f32[3,16,128]{2,1,0:T(8,128)}, f32[16,128]{1,0:T(8,128)}, f32[16,51...) custom-call(bf16[1568,512]{1,0:T(8,128)(2,1)} %bitcast.42, bf16[1568,512]{1,0:T(8,128)(2,1)} %bitcast.43, ...), custom_call_target="tpu_custom_call" | custom-call | tf_op jit(solution)/shard_map/block_forward_backward/pallas_call | solution.py:730
  97.5 5.3 %adam_update.1 = (bf16[1568,512]{1,0:T(8,128)(2,1)}, f32[1568,512]{1,0:T(8,128)}, f32[3,16,128]{2,1,0:T(8,128)}, f32[3,16,128]{2,1,0:T(8,128)}, f32[3,16,128]{2,...) custom-call(bf16[1568,512]{1,0:T(8,128)(2,1)} %get-tuple-element.59., ...), custom_call_target="tpu_custom_call" | custom-call | tf_op jit(solution)/shard_map/adam_update/pallas_call | solution.py:829

commit v3 on v2

--- a/solution.py
+++ b/solution.py
@@ -52,7 +52,7 @@
         return self.device(at)
 
 
-def block_of(ref, lead, place, core, full, axis=None, shift=0):
+def block_of(ref, lead, place, core, full, axis=None, shift=0, half=None):
     whole = slice(None)
     at = list(place.at)
     if axis is not None:
@@ -61,6 +61,7 @@
     x = whole if 0 in full else x
     y = whole if 1 in full else y
     low, high = (whole, whole) if 2 in full else (z % 2, z // 2)
+    low = low if half is None else half
     return ref.at[(*lead, low, core, y, high, x)] if core is not None else ref.at[(*lead, low, y, high, x)]
 
 
@@ -258,6 +259,7 @@
         if n == 1:
             gather_finish(0, 1)
             gather_start(0, 2)
+            gather_finish(1, 1)
 
         def widen(k, _):
             rows = pl.ds(pl.multiple_of(k * 112, 112), 112)
@@ -271,7 +273,8 @@
                 dst[top : top + 7, k * 128 : (k + 1) * 128] = stage[
                     k, pl.ds(first * 8 + image + 2 * t_own, 7, stride=8), :
                 ]
-    gather_finish(1, 1)
+    gather_finish(0, 2, (1, 3))
+    gather_start(1, 2)
 
     def start(k, _):
         rows = pl.ds(pl.multiple_of(k * 64, 64), 64)
@@ -285,6 +288,9 @@
         return 0
 
     lax.fori_loop(0, 8, start, 0)
+    n1_t[...] = n1[...].T
+    cot_t[...] = cot_low[...].T
+    gather_finish(0, 2, (2,))
     for k in range(3):
         wait_in(gs.at[mate_ts[k]], ref.s_out.at[k], ref.s_in.at[k])
     for t in range(4):
@@ -302,11 +308,6 @@
             line = jnp.zeros((16, 128), FULL)
         bias[i * 16 : (i + 1) * 16, :] = jnp.where(low_side, line, BLOCKED)
         bias[(64 + i) * 16 : (65 + i) * 16, :] = jnp.where(high_side, line, BLOCKED)
-    gather_finish(0, 2, (1, 3))
-    gather_start(1, 2)
-    n1_t[...] = n1[...].T
-    cot_t[...] = cot_low[...].T
-    gather_finish(0, 2, (2,))
     gather_last(0)
 
     def columns(b, p, t, a, z):
@@ -328,6 +329,14 @@
         g[b][p, t // 2, t % 2, :, :, :, :, a : a + value.shape[1]] = value.astype(LOW).reshape(
             4, 2, 4, 16, value.shape[1]
         )
+
+    near = ref.near
+
+    def by_head(a):
+        return jnp.concatenate([keep(lane_mask(h), a) for h in range(4)], axis=0)
+
+    def heads_wide(a):
+        return jnp.concatenate([a[h * 128 : (h + 1) * 128] for h in range(4)], axis=1)
 
     def forward(t, _):
         mixed = mm(n1[...], w_qkv(t))
@@ -335,19 +344,16 @@
         qkv[t, 0] = (mixed[:, 0:128] + q_bias).astype(LOW)
         qkv[t, 1] = mixed[:, 128:256].astype(LOW)
         qkv[t, 2] = (mixed[:, 256:384] + v_bias).astype(LOW)
+        for h in range(4):
+            near[h * 128 : (h + 1) * 128, :] = bias[pl.ds(t * 4 + h, 128, stride=16), :]
         for wp in range(4):
             rows = slice(wp * 128, (wp + 1) * 128)
             q, k, v = qkv[t, 0, rows], qkv[t, 1, rows], qkv[t, 2, rows]
-            ps, vs = [], []
-            for h in range(4):
-                mask = lane_mask(h)
-                s = mm_nt(keep(mask, q), k) * SCALE + bias[pl.ds(t * 4 + h, 128, stride=16), :]
-                e = jnp.exp(s - jnp.max(s, axis=-1, keepdims=True))
-                p = (e / jnp.sum(e, axis=-1, keepdims=True)).astype(LOW)
-                probs[t, wp, h] = p
-                ps.append(p)
-                vs.append(keep(mask, v))
-            att[t, rows] = mm(jnp.concatenate(ps, axis=1), jnp.concatenate(vs, axis=0)).astype(LOW)
+            s = mm_nt(by_head(q), k) * SCALE + near[...]
+            e = jnp.exp(s - jnp.max(s, axis=-1, keepdims=True))
+            p = (e * (1.0 / jnp.sum(e, axis=-1, keepdims=True))).astype(LOW)
+            probs[t, wp] = p
+            att[t, rows] = mm(heads_wide(p), by_head(v)).astype(LOW)
         return 0
 
     lax.fori_loop(0, 3, forward, 0)
@@ -358,9 +364,7 @@
 
     def second(k, _):
         rows = pl.ds(pl.multiple_of(k * 128, 128), 128)
-        acc = tok[rows, :] + vec[2:3, :]
-        for t in range(4):
-            acc = acc + mm_nt(att[t, rows, :], w_proj(t))
+        acc = tok[rows, :] + (mid[rows, :] + vec[2:3, :])
         mid[rows, :] = acc
         xs, r = normed(acc)
         x2[rows, :] = xs
@@ -368,65 +372,81 @@
         n2[rows, :] = (xs * (1.0 + vec[3:4, :]) + vec[4:5, :]).astype(LOW)
         return 0
 
+    mid[...] = mm_nt(
+        jnp.concatenate([att[t] for t in range(4)], axis=1), jnp.concatenate([w_proj(t) for t in range(4)], axis=1)
+    )
     lax.fori_loop(0, 4, second, 0)
+    gmid[...] = jnp.zeros((512, 512), FULL)
     n2_t[...] = n2[...].T
+
+    ghid = ref.ghid
 
     def feed(t, _):
         unit = jnp.concatenate([gs[t, 10 + k : 11 + k, :] for k in range(4)], axis=1)
         up_t, down_t = w_up(t), w_down(t)
 
+        tok[...] = mm(n2[...], up_t) + unit
+        ghid[...] = mm(cot_low[...], down_t)
+
         def rows_of(k, total):
-            rows = pl.ds(pl.multiple_of(k * 128, 128), 128)
-            pre = mm(n2[rows, :], up_t) + unit
-            value, slope = gelu_parts(pre)
+            rows = pl.ds(pl.multiple_of(k * 64, 64), 64)
+            value, slope = gelu_parts(tok[rows, :])
             hid[t, rows, :] = value.astype(LOW)
-            grad = mm(cot_low[rows, :], down_t) * slope
+            grad = ghid[rows, :] * slope
             gpre[t, rows, :] = grad.astype(LOW)
             return total + jnp.sum(grad, axis=0, keepdims=True)
 
-        small[pl.ds(8 + t, 1), 0:512] = lax.fori_loop(0, 4, rows_of, jnp.zeros((1, 512), FULL))
+        small[pl.ds(8 + t, 1), 0:512] = lax.fori_loop(0, 8, rows_of, jnp.zeros((1, 512), FULL))
         grad_up = mm(n2_t[...], gpre[t])
         put_grad(1, 0, t, 128, grad_up[:, 0:256])
         put_grad(1, 1, t, 0, grad_up[:, 256:512])
         grad_down = mm(cot_t[...], hid[t])
         put_grad(1, 1, t, 256, grad_down[:, 0:128])
         put_grad(1, 2, t, 0, grad_down[:, 128:512])
+        mid[...] += mm_nt(hid[t], down_t)
+        gmid[...] += mm_nt(gpre[t], up_t)
         return 0
-
-    lax.fori_loop(0, 4, feed, 0)
 
     g_in, g_out, gs_in, gs_out = ref.g_in, ref.g_out, ref.gs_in, ref.gs_out
     slot = ref.slots
 
-    def sum_core(b, p):
+    def sum_core(b, p, half):
         axis, full = SUMS[b][p][0], SUMS[b][p][1:]
         for shift in (1, 3, 2, 0):
-            src = block_of(g[b], (p,), place, 1 - core, full, axis, shift)
-            dst = block_of(sib[b], (p,), place, None, full, axis, shift)
-            send(src, dst, gs_out.at[b, p, shift], gs_in.at[b, p, shift], place.sibling)
+            src = block_of(g[b], (p,), place, 1 - core, full, axis, shift, half)
+            dst = block_of(sib[b], (p,), place, None, full, axis, shift, half)
+            send(src, dst, gs_out.at[b, p, shift, half], gs_in.at[b, p, shift, half], place.sibling)
+
+    def sum_first(b, p, half):
+        axis, full = SUMS[b][p][0], SUMS[b][p][1:]
+        for shift in (1, 3, 2, 0):
+            here = block_of(g[b], (p,), place, core, full, axis, shift, half)
+            there = block_of(sib[b], (p,), place, None, full, axis, shift, half)
+            wait_in(there, gs_out.at[b, p, shift, half], gs_in.at[b, p, shift, half])
+
+            def add(index):
+                here[index] = here[index] + there[index]
+
+            each(block_dims(full)[1:], add)
+            if shift:
+                at = (b, p, 0, shift - 1, half)
+                send(here, slot[b, p, 0].at[shift - 1, half], g_out.at[at], g_in.at[at], place.along(axis, shift))
 
     def sum_start(b, p, phase):
         axis, full = SUMS[b][p][phase], SUMS[b][p][phase + 1 :]
-        for shift in (1, 3, 2, 0):
+        for shift in (1, 3, 2):
             here = block_of(g[b], (p,), place, core, full, axis, shift)
-            if phase == 0:
-                there = block_of(sib[b], (p,), place, None, full, axis, shift)
-                wait_in(there, gs_out.at[b, p, shift], gs_in.at[b, p, shift])
-
-                def add(index):
-                    here[index] = here[index] + there[index]
-
-                each(block_dims(full), add)
-            if shift:
-                at = (b, p, phase, shift - 1)
-                send(here, slot[b, p, phase].at[shift - 1], g_out.at[at], g_in.at[at], place.along(axis, shift))
+            at = (b, p, phase, shift - 1, 0)
+            send(here, slot[b, p, phase].at[shift - 1], g_out.at[at], g_in.at[at], place.along(axis, shift))
 
     def sum_finish(b, p, phase):
         axis, full = SUMS[b][p][phase], SUMS[b][p][phase + 1 :]
         here = block_of(g[b], (p,), place, core, full)
         came = [slot[b, p, phase].at[k] for k in range(3)]
         for k in range(3):
-            wait_in(came[k], g_out.at[b, p, phase, k], g_in.at[b, p, phase, k])
+            for half in range(2 if phase == 0 else 1):
+                at = (b, p, phase, k, half)
+                wait_in(came[k].at[half] if phase == 0 else came[k], g_out.at[at], g_in.at[at])
 
         def total(index):
             one, two, three = (c[index].astype(FULL) for c in came)
@@ -441,17 +461,20 @@
         each(block_dims(full), add)
         return None
 
-    sum_core(1, 1)
-    sum_core(1, 2)
+    lax.fori_loop(0, 2, feed, 0)
+    for p in (1, 2):
+        sum_core(1, p, 0)
+    lax.fori_loop(2, 3, feed, 0)
+    for p in (1, 2):
+        sum_first(1, p, 0)
+    lax.fori_loop(3, 4, feed, 0)
+    for p in (1, 2):
+        sum_core(1, p, 1)
 
     def third(k, _):
         rows = pl.ds(pl.multiple_of(k * 128, 128), 128)
-        out = mid[rows, :] + vec[5:6, :]
-        n = jnp.zeros((128, 512), FULL)
-        for t in range(4):
-            out = out + mm_nt(hid[t, rows, :], w_down(t))
-            n = n + mm_nt(gpre[t, rows, :], w_up(t))
-        mid[rows, :] = out
+        mid[rows, :] += vec[5:6, :]
+        n = gmid[rows, :]
         xs = x2[rows, :]
         grad = cot[rows, :] + norm_back(n, xs, r2[rows, :], vec[3:4, :])
         gmid[rows, :] = grad
@@ -462,6 +485,8 @@
         return 0
 
     lax.fori_loop(0, 4, third, 0)
+    for p in (1, 2):
+        sum_first(1, p, 1)
     gml_t[...] = gml[...].T
 
     def proj_grad(t, _):
@@ -469,7 +494,8 @@
         return 0
 
     lax.fori_loop(0, 4, proj_grad, 0)
-    sum_core(1, 0)
+    for half in range(2):
+        sum_core(1, 0, half)
 
     o_in, o_out = ref.o_in, ref.o_out
 
@@ -509,77 +535,87 @@
             take(n, half, mate_ts[2])
 
     field[...] = jnp.zeros((416, 512), FULL)
-    for p in (1, 2, 0):
-        sum_start(1, p, 0)
     give(0, 0, mid)
     give(0, 1, mid)
-
-    def backward(t, _):
-        ga = mm(gml[...], w_proj(t)).astype(LOW)
-        sums = [jnp.zeros((128, 128), FULL) for _ in range(4)]
+    for half in range(2):
+        sum_first(1, 0, half)
+
+    def backward(image, t):
+        span = slice(image * 256, image * 256 + 256)
+        ga = mm(gml[span, :], w_proj(t)).astype(LOW)
+        sums = jnp.zeros((512, 128), FULL)
         sum_q = jnp.zeros((1, 128), FULL)
         sum_v = jnp.zeros((1, 128), FULL)
-        for wp in range(4):
+        for n in range(2):
+            wp = image * 2 + n
             rows = slice(wp * 128, (wp + 1) * 128)
-            q, k, v, grad = qkv[t, 0, rows], qkv[t, 1, rows], qkv[t, 2, rows], ga[rows]
-            dss, ps, ks, qs, gg = [], [], [], [], []
-            for h in range(4):
-                mask = lane_mask(h)
-                p_low = probs[t, wp, h]
-                p = p_low.astype(FULL)
-                gh = keep(mask, grad)
-                dp = mm_nt(gh, v)
-                ds = (p * (dp - jnp.sum(dp * p, axis=-1, keepdims=True))).astype(LOW)
-                sums[h] = sums[h] + ds.astype(FULL)
-                dss.append(ds)
-                ps.append(p_low)
-                ks.append(keep(mask, k))
-                qs.append(keep(mask, q))
-                gg.append(gh)
-            dq = (mm(jnp.concatenate(dss, axis=1), jnp.concatenate(ks, axis=0)) * SCALE).astype(LOW)
-            dk = (mm_tn(jnp.concatenate(dss, axis=0), jnp.concatenate(qs, axis=0)) * SCALE).astype(LOW)
-            dv = mm_tn(jnp.concatenate(ps, axis=0), jnp.concatenate(gg, axis=0)).astype(LOW)
+            q, k, v = qkv[t, 0, rows], qkv[t, 1, rows], qkv[t, 2, rows]
+            grad = by_head(ga[n * 128 : (n + 1) * 128])
+            p_low = probs[t, wp]
+            p = p_low.astype(FULL)
+            dp = mm_nt(grad, v)
+            ds = (p * (dp - jnp.sum(dp * p, axis=-1, keepdims=True))).astype(LOW)
+            sums = sums + ds.astype(FULL)
+            dq = (mm(heads_wide(ds), by_head(k)) * SCALE).astype(LOW)
+            dk = (mm_tn(ds, by_head(q)) * SCALE).astype(LOW)
+            dv = mm_tn(p_low, grad).astype(LOW)
             dqkv[t, rows, 0:128] = dq
             dqkv[t, rows, 128:256] = dk
             dqkv[t, rows, 256:384] = dv
             sum_q = sum_q + jnp.sum(dq.astype(FULL), axis=0, keepdims=True)
             sum_v = sum_v + jnp.sum(dv.astype(FULL), axis=0, keepdims=True)
         for h in range(4):
-            dsum[pl.ds(t * 4 + h, 128, stride=16), :] = sums[h]
+            at = pl.ds(t * 4 + h, 128, stride=16)
+            value = sums[h * 128 : (h + 1) * 128]
+            dsum[at, :] = value + dsum[at, :] if image else value
         at = pl.ds(pl.multiple_of(t * 128, 128), 128)
-        small[6:7, at] = sum_q
-        small[7:8, at] = sum_v
-        grad = mm(n1_t[...], dqkv[t])
-        for c in range(3):
-            put_grad(0, c, t, 0, grad[:, c * 128 : (c + 1) * 128])
+        small[6:7, at] += sum_q
+        small[7:8, at] += sum_v
+        tok[span, :] += mm_nt(dqkv[t, span, :], w_qkv(t))
+        if image:
+            grad = mm(n1_t[...], dqkv[t])
+            for c in range(3):
+                put_grad(0, c, t, 0, grad[:, c * 128 : (c + 1) * 128])
+
+    def backward_first(t, _):
+        backward(0, t)
         return 0
 
-    lax.fori_loop(0, 4, backward, 0)
+    def backward_second(t, _):
+        backward(1, t)
+        return 0
+
+    def last(k, _):
+        rows = pl.ds(pl.multiple_of(k * 128, 128), 128)
+        n = tok[rows, :]
+        xs = x1[rows, :]
+        gmid[rows, :] += norm_back(n, xs, r1[rows, :], vec[0:1, :])
+        small[0:1, 0:512] += jnp.sum(n * xs, axis=0, keepdims=True)
+        small[1:2, 0:512] += jnp.sum(n, axis=0, keepdims=True)
+        return 0
+
+    tok[...] = jnp.zeros((512, 512), FULL)
+    lax.fori_loop(0, 4, backward_first, 0)
+    lax.fori_loop(0, 2, last, 0)
+    give(1, 0, gmid)
+    lax.fori_loop(0, 2, backward_second, 0)
     for p in range(3):
-        sum_core(0, p)
+        sum_core(0, p, 0)
+    lax.fori_loop(2, 3, backward_second, 0)
+    for p in range(3):
+        sum_first(0, p, 0)
+    lax.fori_loop(3, 4, backward_second, 0)
+    for p in range(3):
+        sum_core(0, p, 1)
+    lax.fori_loop(2, 4, last, 0)
+    give(1, 1, gmid)
+    for p in range(3):
+        sum_first(0, p, 1)
     lines = []
     for i in range(49):
         lines.append(three_lows(dsum[i * 16 : (i + 1) * 16, :] + dsum[(64 + i) * 16 : (65 + i) * 16, :]))
     table_sum = mm_nt(jnp.concatenate(lines, axis=1), onehot[...])
     small[:, 512:768] = table_sum[0:16] + table_sum[16:32] + table_sum[32:48]
-
-    def last(k, _):
-        rows = pl.ds(pl.multiple_of(k * 128, 128), 128)
-        n = jnp.zeros((128, 512), FULL)
-        for t in range(4):
-            n = n + mm_nt(dqkv[t, rows, :], w_qkv(t))
-        xs = x1[rows, :]
-        gmid[rows, :] += norm_back(n, xs, r1[rows, :], vec[0:1, :])
-        small[0:1, 0:512] += jnp.sum(n * xs, axis=0, keepdims=True)
-        small[1:2, 0:512] += jnp.sum(n, axis=0, keepdims=True)
-        return 0
-
-    lax.fori_loop(0, 2, last, 0)
-    give(1, 0, gmid)
-    for p in range(3):
-        sum_start(0, p, 0)
-    lax.fori_loop(2, 4, last, 0)
-    give(1, 1, gmid)
 
     n_in, n_out = ref.n_in, ref.n_out
 
@@ -610,14 +646,15 @@
     small_start(0)
     for half in range(2):
         came(0, half, 1)
+    came(1, 0, 1)
     take_near(0)
-    for p in range(3):
-        sum_finish(1, p, 0)
-        sum_start(1, p, 1)
     for p in range(3):
         sum_finish(0, p, 0)
         sum_start(0, p, 1)
     small_next(0)
+    for p in range(3):
+        sum_finish(1, p, 0)
+        sum_start(1, p, 1)
     take_far(0)
 
     def narrow(k, _):
@@ -635,8 +672,7 @@
         sum_finish(1, p, 1)
         sum_start(1, p, 2)
     take_near(1)
-    for half in range(2):
-        came(1, half, 1)
+    came(1, 1, 1)
     for p in range(3):
         ref.attn_grad[p] = sum_finish(0, p, 2)
     small_next(2)
@@ -689,7 +725,7 @@
         small=pltpu.VMEM((16, 768), FULL),
         steps=pltpu.VMEM((4, 4, 16, 768), FULL),
         qkv=pltpu.VMEM((4, 3, 512, 128), LOW),
-        probs=pltpu.VMEM((4, 4, 4, 128, 128), LOW),
+        probs=pltpu.VMEM((4, 4, 512, 128), LOW),
         att=pltpu.VMEM((4, 512, 128), LOW),
         hid=pltpu.VMEM((4, 512, 512), LOW),
         gpre=pltpu.VMEM((4, 512, 512), LOW),
@@ -700,6 +736,7 @@
         dsum=pltpu.VMEM((2048, 128), FULL),
         table=pltpu.VMEM((16, 256), FULL),
         wide=pltpu.VMEM((56, 128), jnp.int32),
+        near=pltpu.VMEM((512, 128), FULL),
         stage=pltpu.VMEM((4, 1568, 128), FULL),
         field=pltpu.VMEM((416, 512), FULL),
         outs=pltpu.VMEM((2, 4, 416, 512), LOW),
@@ -707,7 +744,7 @@
         r2=pltpu.VMEM((512, 1), FULL),
     )
     full, low = pltpu.VMEM(square, FULL), pltpu.VMEM(square, LOW)
-    scratch.update(tok=full, cot=full, x1=full, x2=full, mid=full, gmid=full)
+    scratch.update(ghid=full, tok=full, cot=full, x1=full, x2=full, mid=full, gmid=full)
     scratch.update(cot_low=low, cot_t=low, n1=low, n1_t=low, n2=low, n2_t=low, gml=low, gml_t=low)
     slots = {}
     for b in range(2):
@@ -716,7 +753,7 @@
                 slots[b, p, phase] = pltpu.VMEM((3, *block_dims(SUMS[b][p][phase + 1 :]), 16, WIDTHS[b]), LOW)
     sems = dict(
         local_sem=(4,), w_in=(2, 3, 3, 3), w_out=(2, 3, 3, 3), ws_in=(2, 3, 4), ws_out=(2, 3, 4),
-        s_in=(3,), s_out=(3,), g_in=(2, 3, 3, 3), g_out=(2, 3, 3, 3), gs_in=(2, 3, 4), gs_out=(2, 3, 4),
+        s_in=(3,), s_out=(3,), g_in=(2, 3, 3, 3, 2), g_out=(2, 3, 3, 3, 2), gs_in=(2, 3, 4, 2), gs_out=(2, 3, 4, 2),
         o_in=(2, 2, 3), o_out=(2, 2, 3), n_in=(4, 3), n_out=(4, 3),
     )
     for name, shape in sems.items():

time: 103 us -> 98.7 us (0.958)
  Pallas kernels: 102 us -> 97.7 us
    pallas_call x1, Pallas kernels: 96.9 us -> 92.4 us  [run_block(): pl.pallas_call(kernel, out_shape=tuple((jax.ShapeDtypeStruct(shape, dtype...]
where the time goes in v3:
time: 98.7 us; the launch traced here: 98.5 us
  Pallas kernels  97.7 us (99%)
    pallas_call x1, Pallas kernels, run_block(): pl.pallas_call(kernel, out_shape=tuple((jax.ShapeDtypeStruct(shape, dtype...  92.4 us
    pallas_call x1, Pallas kernels, update(): pl.pallas_call(update_kernel, out_shape=out_shape, in_specs=[anywhere] *...  5.27 us

profile of v3, /device:TPU:1, one launch (start us, length us, event | category | flops | bytes accessed | tf_op | source)
XLA Modules:
  0.0 98.5 jit_solution(9125520686010932198)
XLA Ops:
  0.7 92.4 %block_forward_backward.1 = (bf16[1568,512]{1,0:T(8,128)(2,1)}, f32[1568,512]{1,0:T(8,128)}, f32[3,16,128]{2,1,0:T(8,128)}, f32[16,128]{1,0:T(8,128)}, f32[16,51...) custom-call(bf16[1568,512]{1,0:T(8,128)(2,1)} %bitcast.42, bf16[1568,512]{1,0:T(8,128)(2,1)} %bitcast.43, ...), custom_call_target="tpu_custom_call" | custom-call | tf_op jit(solution)/shard_map/block_forward_backward/pallas_call | solution.py:767
  93.1 5.3 %adam_update.1 = (bf16[1568,512]{1,0:T(8,128)(2,1)}, f32[1568,512]{1,0:T(8,128)}, f32[3,16,128]{2,1,0:T(8,128)}, f32[3,16,128]{2,1,0:T(8,128)}, f32[3,16,128]{2,...) custom-call(bf16[1568,512]{1,0:T(8,128)(2,1)} %get-tuple-element.59., ...), custom_call_target="tpu_custom_call" | custom-call | tf_op jit(solution)/shard_map/adam_update/pallas_call | solution.py:866

commit v4 on v3

--- a/solution.py
+++ b/solution.py
@@ -226,8 +226,8 @@
                 if phase == 2:
                     send(block, block, sib_out.at[b, p, shift], sib_in.at[b, p, shift], place.sibling)
 
-    def gather_last(b):
-        for p in range(3):
+    def gather_last(b, groups=(0, 1, 2)):
+        for p in groups:
             axis, done = ORDERS[p][2], ORDERS[p][:2]
             for shift in range(4):
                 block = block_of(w[b], (p,), place, 1 - core, done, axis, -shift)
@@ -360,7 +360,7 @@
     gather_finish(1, 2, (1, 3))
     lax.fori_loop(3, 4, forward, 0)
     gather_finish(1, 2, (2,))
-    gather_last(1)
+    gather_last(1, (0,))
 
     def second(k, _):
         rows = pl.ds(pl.multiple_of(k * 128, 128), 128)
@@ -378,6 +378,7 @@
     lax.fori_loop(0, 4, second, 0)
     gmid[...] = jnp.zeros((512, 512), FULL)
     n2_t[...] = n2[...].T
+    gather_last(1, (1, 2))
 
     ghid = ref.ghid
 
@@ -647,11 +648,11 @@
     for half in range(2):
         came(0, half, 1)
     came(1, 0, 1)
-    take_near(0)
     for p in range(3):
         sum_finish(0, p, 0)
         sum_start(0, p, 1)
     small_next(0)
+    take_near(0)
     for p in range(3):
         sum_finish(1, p, 0)
         sum_start(1, p, 1)

time: 98.7 us -> 98.4 us (level)
  no operation moved by 1% of the time
where the time goes in v4:
time: 98.4 us; the launch traced here: 98.2 us
  Pallas kernels  97.4 us (99%)
    pallas_call x1, Pallas kernels, run_block(): pl.pallas_call(kernel, out_shape=tuple((jax.ShapeDtypeStruct(shape, dtype...  92.1 us
    pallas_call x1, Pallas kernels, update(): pl.pallas_call(update_kernel, out_shape=out_shape, in_specs=[anywhere] *...  5.27 us

profile of v4, /device:TPU:1, one launch (start us, length us, event | category | flops | bytes accessed | tf_op | source)
XLA Modules:
  0.0 98.2 jit_solution(4261069311784575465)
XLA Ops:
  0.7 92.1 %block_forward_backward.1 = (bf16[1568,512]{1,0:T(8,128)(2,1)}, f32[1568,512]{1,0:T(8,128)}, f32[3,16,128]{2,1,0:T(8,128)}, f32[16,128]{1,0:T(8,128)}, f32[16,51...) custom-call(bf16[1568,512]{1,0:T(8,128)(2,1)} %bitcast.42, bf16[1568,512]{1,0:T(8,128)(2,1)} %bitcast.43, ...), custom_call_target="tpu_custom_call" | custom-call | tf_op jit(solution)/shard_map/block_forward_backward/pallas_call | solution.py:768
  92.8 5.3 %adam_update.1 = (bf16[1568,512]{1,0:T(8,128)(2,1)}, f32[1568,512]{1,0:T(8,128)}, f32[3,16,128]{2,1,0:T(8,128)}, f32[3,16,128]{2,1,0:T(8,128)}, f32[3,16,128]{2,...) custom-call(bf16[1568,512]{1,0:T(8,128)(2,1)} %get-tuple-element.59., ...), custom_call_target="tpu_custom_call" | custom-call | tf_op jit(solution)/shard_map/adam_update/pallas_call | solution.py:867
